TPU v7x, 32 devices: a whole 2x2x4 slice. The times are simulated.
32 devices in a mesh: groups: 2 (over y), gx: 4 (over z), gy: 4 (over x, core).
Axes of the slice: x: 2, y: 2, z: 4, core: 2. Of those that a mesh axis runs over, the one named last changes fastest.
Arguments:
- velocity: float32 [3, 64, 64, 128], P(None, ('groups', 'gx'), 'gy'), parts along dimension 1, may hold values from -6 to 6
- viscosity: float32 [64, 64, 128], P(('groups', 'gx'), 'gy'), parts along dimension 0, may hold values from 0.1 to 3
- marker_force: float32 [256, 3, 128], P(('groups', 'gx', 'gy')), parts along dimension 0, may hold values from -300 to 300
- delta_weights: float32 [256, 3, 4, 128], P(('groups', 'gx', 'gy')), parts along dimension 0, may hold values from 0 to 0.5, as said below
- marker_cells: int32 [256, 3, 128], P(('groups', 'gx', 'gy')), parts along dimension 0, may hold values from 0 to 127, as said below
- block_count: int32 [256], P(('groups', 'gx', 'gy')), parts along dimension 0, may hold values from 1 to 128, as said below
- destination: int32 [256], P(('groups', 'gx', 'gy')), parts along dimension 0, may hold values from 0 to 15, as said below
Outputs:
- flow: float32 [3, 64, 64, 128], P(None, ('groups', 'gx'), 'gy'), parts along dimension 1
- marker_velocity: float32 [256, 3, 128], P(('groups', 'gx', 'gy')), parts along dimension 0
There are 2 independent parts, one for each index of `groups`. A program takes and returns all parts, laid end to end along the dimension named above; each array names one. Nothing has to cross between parts.
Inputs may be any that keep to these rules, and one draw needn't show every extreme that they name: A block's destination is its source device or one of the eight devices at most one index away along gx and along gy, with wrap-around; the source of block k is device k // 8, and a flat index is the gx index times the size of gy plus the gy index. At most 2 blocks of one device go to one destination, every device keeps at least one of its blocks, every device sends exactly 2 to one of them, and in every draw some device receives 2 blocks from each of its nine sources. `marker_cells`: components are below 8, 16 and 128 for x, y and z. `block_count`: markers at or beyond the count are padding; their data are arbitrary. `delta_weights`: peskin four-point weights of a marker's fractional offset along each direction; the four weights of one direction sum to one.
All inputs are finite; a program needn't handle non-finite values.
Results may differ from a plain program's by a relative error of at most 0.00013.
Values sent between devices are 32-bit elements; how exact they have to be, the bound alone decides.
A program may use at most 64 MiB of HBM per device.

v0:
```python
import jax
import jax.numpy as jnp
from jax import lax
from jax.sharding import PartitionSpec as P

CAP = 2
SWEEPS = 8


KAPPA = 2.0


def extended(shard, sides, width):
    for axis, dim in sides:
        peers, length = (lax.axis_size(axis), shard.shape[dim])
        up = [(i, (i + 1) % peers) for i in range(peers)]
        down = [(j, i) for i, j in up]
        last = lax.slice_in_dim(shard, length - width, length, axis=dim)
        initial = lax.slice_in_dim(shard, 0, width, axis=dim)
        before = lax.ppermute(last, axis, up)
        after = lax.ppermute(initial, axis, down)
        shard = jnp.concatenate([before, shard, after], axis=dim)
    return shard


def parity_grid(extent_x, extent_y, depth_z):
    shape = (extent_x, extent_y, depth_z)
    return (
        lax.broadcasted_iota(jnp.int32, shape, 0)
        + lax.broadcasted_iota(jnp.int32, shape, 1)
        + lax.broadcasted_iota(jnp.int32, shape, 2)
    ) % 2


def coefficients(visc_pad):
    centre = visc_pad[1:-1, 1:-1]
    face_east = 0.5 * (centre + visc_pad[2:, 1:-1])
    face_west = 0.5 * (centre + visc_pad[:-2, 1:-1])
    face_north = 0.5 * (centre + visc_pad[1:-1, 2:])
    face_south = 0.5 * (centre + visc_pad[1:-1, :-2])
    face_up = 0.5 * (centre + jnp.roll(centre, -1, 2))
    face_down = 0.5 * (centre + jnp.roll(centre, 1, 2))
    diagonal = 1.0 + KAPPA * (face_east + face_west + face_north + face_south + face_up + face_down)
    return ((face_east, face_west, face_north, face_south, face_up, face_down), diagonal)


def relax_cells(state_pad, faces, diagonal, source_term, chosen):
    face_east, face_west, face_north, face_south, face_up, face_down = faces
    centre = state_pad[:, 1:-1, 1:-1]
    summed = (
        face_east * state_pad[:, 2:, 1:-1]
        + face_west * state_pad[:, :-2, 1:-1]
        + face_north * state_pad[:, 1:-1, 2:]
        + face_south * state_pad[:, 1:-1, :-2]
        + face_up * jnp.roll(centre, -1, 3)
        + face_down * jnp.roll(centre, 1, 3)
    )
    return jnp.where(chosen, (source_term + KAPPA * summed) / diagonal, centre)


def slot_tables(weights, stencil_cells, extent_x, extent_y, depth_z):
    plane_x = lax.broadcasted_iota(jnp.int32, (extent_x, weights.shape[2]), 0)
    plane_y = lax.broadcasted_iota(jnp.int32, (extent_y, weights.shape[2]), 0)
    plane_z = lax.broadcasted_iota(jnp.int32, (depth_z, weights.shape[2]), 0)
    table_x = jnp.zeros((extent_x, weights.shape[2]), jnp.float32)
    table_y = jnp.zeros((extent_y, weights.shape[2]), jnp.float32)
    table_z = jnp.zeros((depth_z, weights.shape[2]), jnp.float32)
    for offset in range(4):
        table_x = table_x + jnp.where(
            plane_x == stencil_cells[0] + (offset + 1), weights[0, offset], 0.0
        )
        table_y = table_y + jnp.where(
            plane_y == stencil_cells[1] + (offset + 1), weights[1, offset], 0.0
        )
        table_z = table_z + jnp.where(
            plane_z == (stencil_cells[2] + (offset - 1)) % depth_z, weights[2, offset], 0.0
        )
    table_xy = (table_x[:, None, :] * table_y[None, :, :]).reshape(extent_x * extent_y, -1)
    return (table_xy, table_z)


def local(velocity, viscosity, marker_force, delta_weights, marker_cells, block_count, destination):
    cells_x, cells_y, depth_z = viscosity.shape
    block_total, marker_total = (block_count.shape[0], marker_force.shape[2])
    extent_x, extent_y = (cells_x + 4, cells_y + 4)
    size_x = lax.axis_size("gx")
    size_y = lax.axis_size("gy")
    here_x = lax.axis_index("gx")
    here_y = lax.axis_index("gy")
    live_mask = (
        lax.broadcasted_iota(jnp.int32, (block_total, marker_total), 1) < block_count[:, None]
    ).astype(jnp.float32)
    packed = jnp.concatenate(
        [
            marker_force * live_mask[:, None, :],
            delta_weights.reshape(block_total, 12, marker_total),
            marker_cells.astype(jnp.float32),
        ],
        axis=1,
    )
    step_x = (destination // size_y - here_x + 1) % size_x
    step_y = (destination % size_y - here_y + 1) % size_y
    earlier = lax.broadcasted_iota(jnp.int32, (block_total, block_total), 1) < lax.broadcasted_iota(
        jnp.int32, (block_total, block_total), 0
    )
    slot_rank = jnp.sum((destination[:, None] == destination[None, :]) & earlier, axis=1)
    target = (step_x * 3 + step_y) * CAP + slot_rank
    onehot = (target[:, None] == jnp.arange(9 * CAP, dtype=jnp.int32)[None, :]).astype(jnp.float32)
    outgoing = jnp.dot(
        onehot.T,
        packed.reshape(block_total, -1),
        precision=lax.Precision.HIGHEST,
        preferred_element_type=jnp.float32,
    ).reshape(3, 3, CAP, 18, marker_total)
    arrived = extended(outgoing, (("gx", 0), ("gy", 1)), 1)[0::2, 0::2]
    arrived = arrived.reshape(9 * CAP, 18, marker_total)
    slot_force = arrived[:, 0:3]
    slot_weights = arrived[:, 3:15].reshape(9 * CAP, 3, 4, marker_total)
    slot_cells = arrived[:, 15:18].astype(jnp.int32)

    def spread_block(total, inputs):
        force_block, weight_block, cell_block = inputs
        table_xy, table_z = slot_tables(weight_block, cell_block, extent_x, extent_y, depth_z)
        left = (force_block[:, None, :] * table_xy[None]).reshape(3 * extent_x * extent_y, -1)
        total = total + jnp.dot(
            left, table_z.T, precision=lax.Precision.HIGHEST, preferred_element_type=jnp.float32
        )
        return (total, None)

    spread_init = jnp.zeros((3 * extent_x * extent_y, depth_z), jnp.float32)
    spread_grid, unused = lax.scan(
        spread_block, spread_init, (slot_force, slot_weights, slot_cells)
    )
    spread_grid = spread_grid.reshape(3, extent_x, extent_y, depth_z)
    strips_x = jnp.concatenate([spread_grid[:, :2], spread_grid[:, -2:]], axis=1)
    got_x = extended(strips_x, (("gx", 1),), 2)
    middle = spread_grid[:, 2:-2]
    middle = middle.at[:, :2].add(got_x[:, :2]).at[:, -2:].add(got_x[:, -2:])
    strips_y = jnp.concatenate([middle[:, :, :2], middle[:, :, -2:]], axis=2)
    got_y = extended(strips_y, (("gy", 2),), 2)
    forcing = middle[:, :, 2:-2]
    forcing = forcing.at[:, :, :2].add(got_y[:, :, :2]).at[:, :, -2:].add(got_y[:, :, -2:])
    source_term = velocity + forcing
    visc_pad = extended(viscosity, (("gx", 0), ("gy", 1)), 2)
    faces_inner, diagonal_inner = coefficients(visc_pad[1:-1, 1:-1])
    colours_inner = parity_grid(cells_x, cells_y, depth_z)
    current = velocity
    for sweep_index in range(SWEEPS):
        for colour in range(2):
            padded = extended(current, (("gx", 1), ("gy", 2)), 1)
            current = relax_cells(
                padded, faces_inner, diagonal_inner, source_term, colours_inner == colour
            )
    final_pad = extended(current, (("gx", 1), ("gy", 2)), 2)
    field_rows = final_pad.reshape(3 * extent_x * extent_y, depth_z)

    def sample_block(carry, inputs):
        weight_block, cell_block = inputs
        table_xy, table_z = slot_tables(weight_block, cell_block, extent_x, extent_y, depth_z)
        picked = jnp.dot(
            field_rows, table_z, precision=lax.Precision.HIGHEST, preferred_element_type=jnp.float32
        ).reshape(3, extent_x * extent_y, -1)
        return (carry, jnp.sum(picked * table_xy[None], axis=1))

    unused_carry, results = lax.scan(
        sample_block, jnp.zeros((), jnp.float32), (slot_weights, slot_cells)
    )
    results = results.reshape(3, 3, CAP, 3, marker_total)
    returned = extended(results, (("gx", 0), ("gy", 1)), 1)[0::2, 0::2]
    returned_own = jnp.dot(
        onehot,
        returned.reshape(9 * CAP, -1),
        precision=lax.Precision.HIGHEST,
        preferred_element_type=jnp.float32,
    ).reshape(block_total, 3, marker_total)
    return (current, returned_own * live_mask[:, None, :])


def solution(mesh):
    return jax.shard_map(
        local,
        mesh=mesh,
        in_specs=(
            P(None, ("groups", "gx"), "gy", None),
            P(("groups", "gx"), "gy", None),
            P(("groups", "gx", "gy"), None, None),
            P(("groups", "gx", "gy"), None, None, None),
            P(("groups", "gx", "gy"), None, None),
            P(("groups", "gx", "gy")),
            P(("groups", "gx", "gy")),
        ),
        out_specs=(P(None, ("groups", "gx"), "gy", None), P(("groups", "gx", "gy"), None, None)),
        check_vma=False,
    )
```

profile of v0, /device:TPU:1, one launch (start us, length us, event | category | flops | bytes accessed | tf_op | source)
XLA Modules:
  0.0 230.9 jit_solution(10948232675694302742)
XLA Ops:
  4.0 2.2 collective-permute-start
  6.2 2.1 collective-permute-start.1
  8.3 3.3 %collective-permute-start.8 = (f32[2,16,128]{2,1,0:T(8,128)S(1)}, f32[2,16,128]{2,1,0:T(8,128)S(1)}, u32[]{:S(2)}, u32[]{:S(2)}) collective-permute-start(f32[2,16,128]{2,1,0:T(8,128)S(1)} %get-tuple-element.427), channel_id=1, source_target_pairs={{4,0},{8,4},{12,8},{0,12},{5,1},{9,5},{13,9},{1,13},{6,2},{10,6},{... | collective-permute-start | bytes 49160 | tf_op jit(solution)/shard_map/ppermute | solution.py:21
  12.8 2.6 %collective-permute-start.9 = (f32[3,1,16,128]{3,2,1,0:T(8,128)S(1)}, f32[3,1,16,128]{3,2,1,0:T(8,128)S(1)}, u32[]{:S(2)}, u32[]{:S(2)}) collective-permute-start(f32[3,1,16,128]{3,2,1,0:T(8,128)S(1)} %get-tuple-element.419), channel_id=1, source_target_pairs={{4,0},{8,4},{12,8},{0,12},{5,1},{9,5},{13,9},{1,13},{6,2},{10,6},{... | collective-permute-start | bytes 73736 | tf_op jit(solution)/shard_map/ppermute | solution.py:21
  15.5 2.1 collective-permute-start.12
  17.6 2.4 %collective-permute-start.14 = (f32[12,2,128]{2,1,0:T(2,128)S(1)}, f32[12,2,128]{2,1,0:T(2,128)S(1)}, u32[]{:S(2)}, u32[]{:S(2)}) collective-permute-start(f32[12,2,128]{2,1,0:T(2,128)S(1)} %get-tuple-element.421), channel_id=1, source_target_pairs={{0,1},{1,2},{2,3},{3,0},{4,5},{5,6},{6,7},{7,4},{8,9},{9,10},{10,1... | collective-permute-start | bytes 36872 | tf_op jit(solution)/shard_map/ppermute | solution.py:20
  24.8 15.6 %while.30 = (s32[]{:T(128)}, f32[720,128]{1,0:T(8,128)S(1)}, f32[18,3,128]{2,1,0:T(4,128)S(1)}, s32[18,3,128]{2,1,0:T(4,128)S(1)}, f32[18,3,4,128]{3,2,1,0:T(4,128)S(1)}, /*index=5*/s32[]{:T(128)}, s32[]{:T(128)}) while((s32[]{:T(128)}, f32[720,128]{1,0:T(8,128)S(1)}, f32[18,3,128]{2,1,0:T(4,128)S(1)}, ...), condition=%wide.region_2.3_spmd.clone, body=%wide.region_1.2_spmd.clone.sunk | while | flops 142097280 | bytes 2051171 | solution.py:131
  42.4 3.6 %collective-permute-done.4 = f32[3,2,20,128]{3,2,1,0:T(8,128)S(1)} collective-permute-done((f32[3,2,20,128]{3,2,1,0:T(8,128)S(1)}, f32[3,2,20,128]{3,2,1,0:T(8,128)S(1)}, u32[]{:S(2)}, u32[]{:S(2)}) %collective-permute-start.4) | collective-permute-done | bytes 61472 | tf_op jit(solution)/shard_map/ppermute | solution.py:20
  46.0 3.2 %collective-permute-done.5 = f32[3,2,20,128]{3,2,1,0:T(8,128)S(1)} collective-permute-done((f32[3,2,20,128]{3,2,1,0:T(8,128)S(1)}, f32[3,2,20,128]{3,2,1,0:T(8,128)S(1)}, u32[]{:S(2)}, u32[]{:S(2)}) %collective-permute-start.5) | collective-permute-done | bytes 61472 | tf_op jit(solution)/shard_map/ppermute | solution.py:21
  49.2 2.8 %collective-permute-start.6 = (f32[3,8,2,128]{3,2,1,0:T(2,128)S(1)}, f32[3,8,2,128]{3,2,1,0:T(2,128)S(1)}, u32[]{:S(2)}, u32[]{:S(2)}) collective-permute-start(f32[3,8,2,128]{3,2,1,0:T(2,128)S(1)} %get-tuple-element.286), channel_id=1, source_target_pairs={{0,1},{1,2},{2,3},{3,0},{4,5},{5,6},{6,7},{7,4},{8,9},{9,10},{10,1... | collective-permute-start | bytes 73736 | tf_op jit(solution)/shard_map/ppermute | solution.py:20
  53.0 2.5 %collective-permute-done.7 = f32[3,8,2,128]{3,2,1,0:T(2,128)S(1)} collective-permute-done((f32[3,8,2,128]{3,2,1,0:T(2,128)S(1)}, f32[3,8,2,128]{3,2,1,0:T(2,128)S(1)}, u32[]{:S(2)}, u32[]{:S(2)}) %collective-permute-start.7) | collective-permute-done | bytes 24608 | tf_op jit(solution)/shard_map/ppermute | solution.py:21
  58.5 3.4 %collective-permute-done.17 = f32[3,1,16,128]{3,2,1,0:T(8,128)S(1)} collective-permute-done((f32[3,1,16,128]{3,2,1,0:T(8,128)S(1)}, f32[3,1,16,128]{3,2,1,0:T(8,128)S(1)}, u32[]{:S(2)}, u32[]{:S(2)}) %collective-permute-start.17) | collective-permute-done | bytes 24608 | tf_op jit(solution)/shard_map/ppermute | solution.py:20
  70.5 2.0 collective-permute-start.22
  79.4 2.3 %collective-permute-start.26 = (f32[3,10,1,128]{3,2,1,0:T(1,128)S(1)}, f32[3,10,1,128]{3,2,1,0:T(1,128)S(1)}, u32[]{:S(2)}, u32[]{:S(2)}) collective-permute-start(f32[3,10,1,128]{3,2,1,0:T(1,128)S(1)} %get-tuple-element.311), channel_id=1, source_target_pairs={{1,0},{2,1},{3,2},{0,3},{5,4},{6,5},{7,6},{4,7},{9,8},{10,9},{11,1... | collective-permute-start | bytes 46088 | tf_op jit(solution)/shard_map/ppermute | solution.py:21
  88.7 2.3 %collective-permute-start.30 = (f32[3,10,1,128]{3,2,1,0:T(1,128)S(1)}, f32[3,10,1,128]{3,2,1,0:T(1,128)S(1)}, u32[]{:S(2)}, u32[]{:S(2)}) collective-permute-start(f32[3,10,1,128]{3,2,1,0:T(1,128)S(1)} %get-tuple-element.309), channel_id=1, source_target_pairs={{1,0},{2,1},{3,2},{0,3},{5,4},{6,5},{7,6},{4,7},{9,8},{10,9},{11,1... | collective-permute-start | bytes 46088 | tf_op jit(solution)/shard_map/ppermute | solution.py:21
  98.1 2.3 %collective-permute-start.34 = (f32[3,10,1,128]{3,2,1,0:T(1,128)S(1)}, f32[3,10,1,128]{3,2,1,0:T(1,128)S(1)}, u32[]{:S(2)}, u32[]{:S(2)}) collective-permute-start(f32[3,10,1,128]{3,2,1,0:T(1,128)S(1)} %get-tuple-element.307), channel_id=1, source_target_pairs={{1,0},{2,1},{3,2},{0,3},{5,4},{6,5},{7,6},{4,7},{9,8},{10,9},{11,1... | collective-permute-start | bytes 46088 | tf_op jit(solution)/shard_map/ppermute | solution.py:21
  107.4 2.4 %collective-permute-start.38 = (f32[3,10,1,128]{3,2,1,0:T(1,128)S(1)}, f32[3,10,1,128]{3,2,1,0:T(1,128)S(1)}, u32[]{:S(2)}, u32[]{:S(2)}) collective-permute-start(f32[3,10,1,128]{3,2,1,0:T(1,128)S(1)} %get-tuple-element.305), channel_id=1, source_target_pairs={{1,0},{2,1},{3,2},{0,3},{5,4},{6,5},{7,6},{4,7},{9,8},{10,9},{11,1... | collective-permute-start | bytes 46088 | tf_op jit(solution)/shard_map/ppermute | solution.py:21
  116.7 2.5 %collective-permute-start.42 = (f32[3,10,1,128]{3,2,1,0:T(1,128)S(1)}, f32[3,10,1,128]{3,2,1,0:T(1,128)S(1)}, u32[]{:S(2)}, u32[]{:S(2)}) collective-permute-start(f32[3,10,1,128]{3,2,1,0:T(1,128)S(1)} %get-tuple-element.303), channel_id=1, source_target_pairs={{1,0},{2,1},{3,2},{0,3},{5,4},{6,5},{7,6},{4,7},{9,8},{10,9},{11,1... | collective-permute-start | bytes 46088 | tf_op jit(solution)/shard_map/ppermute | solution.py:21
  126.2 2.4 %collective-permute-start.46 = (f32[3,10,1,128]{3,2,1,0:T(1,128)S(1)}, f32[3,10,1,128]{3,2,1,0:T(1,128)S(1)}, u32[]{:S(2)}, u32[]{:S(2)}) collective-permute-start(f32[3,10,1,128]{3,2,1,0:T(1,128)S(1)} %get-tuple-element.301), channel_id=1, source_target_pairs={{1,0},{2,1},{3,2},{0,3},{5,4},{6,5},{7,6},{4,7},{9,8},{10,9},{11,1... | collective-permute-start | bytes 46088 | tf_op jit(solution)/shard_map/ppermute | solution.py:21
  135.6 2.5 %collective-permute-start.50 = (f32[3,10,1,128]{3,2,1,0:T(1,128)S(1)}, f32[3,10,1,128]{3,2,1,0:T(1,128)S(1)}, u32[]{:S(2)}, u32[]{:S(2)}) collective-permute-start(f32[3,10,1,128]{3,2,1,0:T(1,128)S(1)} %get-tuple-element.299), channel_id=1, source_target_pairs={{1,0},{2,1},{3,2},{0,3},{5,4},{6,5},{7,6},{4,7},{9,8},{10,9},{11,1... | collective-permute-start | bytes 46088 | tf_op jit(solution)/shard_map/ppermute | solution.py:21
  144.9 2.5 %collective-permute-start.54 = (f32[3,10,1,128]{3,2,1,0:T(1,128)S(1)}, f32[3,10,1,128]{3,2,1,0:T(1,128)S(1)}, u32[]{:S(2)}, u32[]{:S(2)}) collective-permute-start(f32[3,10,1,128]{3,2,1,0:T(1,128)S(1)} %get-tuple-element.297), channel_id=1, source_target_pairs={{1,0},{2,1},{3,2},{0,3},{5,4},{6,5},{7,6},{4,7},{9,8},{10,9},{11,1... | collective-permute-start | bytes 46088 | tf_op jit(solution)/shard_map/ppermute | solution.py:21
  154.4 2.6 %collective-permute-start.58 = (f32[3,10,1,128]{3,2,1,0:T(1,128)S(1)}, f32[3,10,1,128]{3,2,1,0:T(1,128)S(1)}, u32[]{:S(2)}, u32[]{:S(2)}) collective-permute-start(f32[3,10,1,128]{3,2,1,0:T(1,128)S(1)} %get-tuple-element.295), channel_id=1, source_target_pairs={{1,0},{2,1},{3,2},{0,3},{5,4},{6,5},{7,6},{4,7},{9,8},{10,9},{11,1... | collective-permute-start | bytes 46088 | tf_op jit(solution)/shard_map/ppermute | solution.py:21
  164.0 2.3 %collective-permute-start.62 = (f32[3,10,1,128]{3,2,1,0:T(1,128)S(1)}, f32[3,10,1,128]{3,2,1,0:T(1,128)S(1)}, u32[]{:S(2)}, u32[]{:S(2)}) collective-permute-start(f32[3,10,1,128]{3,2,1,0:T(1,128)S(1)} %get-tuple-element.293), channel_id=1, source_target_pairs={{1,0},{2,1},{3,2},{0,3},{5,4},{6,5},{7,6},{4,7},{9,8},{10,9},{11,1... | collective-permute-start | bytes 46088 | tf_op jit(solution)/shard_map/ppermute | solution.py:21
  173.2 2.4 %collective-permute-start.66 = (f32[3,10,1,128]{3,2,1,0:T(1,128)S(1)}, f32[3,10,1,128]{3,2,1,0:T(1,128)S(1)}, u32[]{:S(2)}, u32[]{:S(2)}) collective-permute-start(f32[3,10,1,128]{3,2,1,0:T(1,128)S(1)} %get-tuple-element.291), channel_id=1, source_target_pairs={{1,0},{2,1},{3,2},{0,3},{5,4},{6,5},{7,6},{4,7},{9,8},{10,9},{11,1... | collective-permute-start | bytes 46088 | tf_op jit(solution)/shard_map/ppermute | solution.py:21
  182.6 2.5 %collective-permute-start.70 = (f32[3,10,1,128]{3,2,1,0:T(1,128)S(1)}, f32[3,10,1,128]{3,2,1,0:T(1,128)S(1)}, u32[]{:S(2)}, u32[]{:S(2)}) collective-permute-start(f32[3,10,1,128]{3,2,1,0:T(1,128)S(1)} %get-tuple-element.289), channel_id=1, source_target_pairs={{1,0},{2,1},{3,2},{0,3},{5,4},{6,5},{7,6},{4,7},{9,8},{10,9},{11,1... | collective-permute-start | bytes 46088 | tf_op jit(solution)/shard_map/ppermute | solution.py:21
  192.0 2.4 %collective-permute-start.74 = (f32[3,10,1,128]{3,2,1,0:T(1,128)S(1)}, f32[3,10,1,128]{3,2,1,0:T(1,128)S(1)}, u32[]{:S(2)}, u32[]{:S(2)}) collective-permute-start(f32[3,10,1,128]{3,2,1,0:T(1,128)S(1)} %get-tuple-element.287), channel_id=1, source_target_pairs={{1,0},{2,1},{3,2},{0,3},{5,4},{6,5},{7,6},{4,7},{9,8},{10,9},{11,1... | collective-permute-start | bytes 46088 | tf_op jit(solution)/shard_map/ppermute | solution.py:21
  196.8 3.3 %collective-permute-start.77 = (f32[3,2,16,128]{3,2,1,0:T(8,128)S(1)}, f32[3,2,16,128]{3,2,1,0:T(8,128)S(1)}, u32[]{:S(2)}, u32[]{:S(2)}) collective-permute-start(f32[3,2,16,128]{3,2,1,0:T(8,128)S(1)} %get-tuple-element.324), channel_id=1, source_target_pairs={{4,0},{8,4},{12,8},{0,12},{5,1},{9,5},{13,9},{1,13},{6,2},{10,6},{... | collective-permute-start | bytes 147464 | tf_op jit(solution)/shard_map/ppermute | solution.py:21
  201.7 2.9 %collective-permute-start.78 = (f32[3,12,2,128]{3,2,1,0:T(2,128)S(1)}, f32[3,12,2,128]{3,2,1,0:T(2,128)S(1)}, u32[]{:S(2)}, u32[]{:S(2)}) collective-permute-start(f32[3,12,2,128]{3,2,1,0:T(2,128)S(1)} %get-tuple-element.283), channel_id=1, source_target_pairs={{0,1},{1,2},{2,3},{3,0},{4,5},{5,6},{6,7},{7,4},{8,9},{9,10},{10,1... | collective-permute-start | bytes 110600 | tf_op jit(solution)/shard_map/ppermute | solution.py:20
  205.6 2.3 %collective-permute-done.79 = f32[3,12,2,128]{3,2,1,0:T(2,128)S(1)} collective-permute-done((f32[3,12,2,128]{3,2,1,0:T(2,128)S(1)}, f32[3,12,2,128]{3,2,1,0:T(2,128)S(1)}, u32[]{:S(2)}, u32[]{:S(2)}) %collective-permute-start.79) | collective-permute-done | bytes 36896 | tf_op jit(solution)/shard_map/ppermute | solution.py:21
  208.1 13.1 %while.29 = (s32[]{:T(128)}, f32[18,3,128]{2,1,0:T(4,128)S(1)}, s32[18,3,128]{2,1,0:T(4,128)S(1)}, f32[18,3,4,128]{3,2,1,0:T(4,128)S(1)}, f32[720,128]{1,0:T(8,128)S(1)}, /*index=5*/s32[]{:T(128)}) while((s32[]{:T(128)}, f32[18,3,128]{2,1,0:T(4,128)S(1)}, s32[18,3,128]{2,1,0:T(4,128)S(1)}, f32[18,3,4,128]{3,2,1,0:T(4,128)S(1)}, ...), condition=%wide.region_5.6_spmd, body=%wide.region_3.5_spmd.sunk | while | flops 142004736 | bytes 1683537 | solution.py:165
  221.3 3.6 %collective-permute-start.81 = (f32[1,3,2,3,128]{4,3,2,1,0:T(4,128)S(1)}, f32[1,3,2,3,128]{4,3,2,1,0:T(4,128)S(1)}, u32[]{:S(2)}, u32[]{:S(2)}) collective-permute-start(f32[1,3,2,3,128]{4,3,2,1,0:T(4,128)S(1)} %bitcast.173), channel_id=1, source_target_pairs={{4,0},{8,4},{12,8},{0,12},{5,1},{9,5},{13,9},{1,13},{6,2},{10,6},{... | collective-permute-start | bytes 27656 | tf_op jit(solution)/shard_map/ppermute | solution.py:21
  227.7 2.3 collective-permute-done.83
  (720 shorter events, 147.6 us)
Async XLA Ops:
  4.0 16.1 %collective-permute-start = (f32[1,3,2,18,128]{4,3,2,1,0:T(8,128)S(1)}, f32[1,3,2,18,128]{4,3,2,1,0:T(8,128)S(1)}, u32[]{:S(2)}, u32[]{:S(2)}) collective-permute-start(f32[1,3,2,18,128]{4,3,2,1,0:T(8,128)S(1)} %slice.1102), channel_id=1, source_target_pairs={{0,4},{4,8},{8,12},{12,0},{1,5},{5,9},{9,13},{13,1},{2,6},{6,10},{... | collective-permute-start | bytes 165896 | tf_op jit(solution)/shard_map/ppermute | solution.py:20
  6.2 13.9 %collective-permute-start.1 = (f32[1,3,2,18,128]{4,3,2,1,0:T(8,128)S(1)}, f32[1,3,2,18,128]{4,3,2,1,0:T(8,128)S(1)}, u32[]{:S(2)}, u32[]{:S(2)}) collective-permute-start(f32[1,3,2,18,128]{4,3,2,1,0:T(8,128)S(1)} %slice.1104), channel_id=1, source_target_pairs={{4,0},{8,4},{12,8},{0,12},{5,1},{9,5},{13,9},{1,13},{6,2},{10,6},{... | collective-permute-start | bytes 165896 | tf_op jit(solution)/shard_map/ppermute | solution.py:21
  8.3 7.1 %collective-permute-start.8 = (f32[2,16,128]{2,1,0:T(8,128)S(1)}, f32[2,16,128]{2,1,0:T(8,128)S(1)}, u32[]{:S(2)}, u32[]{:S(2)}) collective-permute-start(f32[2,16,128]{2,1,0:T(8,128)S(1)} %get-tuple-element.427), channel_id=1, source_target_pairs={{4,0},{8,4},{12,8},{0,12},{5,1},{9,5},{13,9},{1,13},{6,2},{10,6},{... | collective-permute-start | bytes 49160 | tf_op jit(solution)/shard_map/ppermute | solution.py:21
  11.6 6.0 %collective-permute-start.11 = (f32[3,1,16,128]{3,2,1,0:T(8,128)S(1)}, f32[3,1,16,128]{3,2,1,0:T(8,128)S(1)}, u32[]{:S(2)}, u32[]{:S(2)}) collective-permute-start(f32[3,1,16,128]{3,2,1,0:T(8,128)S(1)} %get-tuple-element.420), channel_id=1, source_target_pairs={{0,4},{4,8},{8,12},{12,0},{1,5},{5,9},{9,13},{13,1},{2,6},{6,10},{... | collective-permute-start | bytes 73736 | tf_op jit(solution)/shard_map/ppermute | solution.py:20
  12.8 7.9 %collective-permute-start.9 = (f32[3,1,16,128]{3,2,1,0:T(8,128)S(1)}, f32[3,1,16,128]{3,2,1,0:T(8,128)S(1)}, u32[]{:S(2)}, u32[]{:S(2)}) collective-permute-start(f32[3,1,16,128]{3,2,1,0:T(8,128)S(1)} %get-tuple-element.419), channel_id=1, source_target_pairs={{4,0},{8,4},{12,8},{0,12},{5,1},{9,5},{13,9},{1,13},{6,2},{10,6},{... | collective-permute-start | bytes 73736 | tf_op jit(solution)/shard_map/ppermute | solution.py:21
  15.5 36.5 %collective-permute-start.12 = (f32[12,2,128]{2,1,0:T(2,128)S(1)}, f32[12,2,128]{2,1,0:T(2,128)S(1)}, u32[]{:S(2)}, u32[]{:S(2)}) collective-permute-start(f32[12,2,128]{2,1,0:T(2,128)S(1)} %get-tuple-element.422), channel_id=1, source_target_pairs={{1,0},{2,1},{3,2},{0,3},{5,4},{6,5},{7,6},{4,7},{9,8},{10,9},{11,1... | collective-permute-start | bytes 36872 | tf_op jit(solution)/shard_map/ppermute | solution.py:21
  17.6 34.4 %collective-permute-start.14 = (f32[12,2,128]{2,1,0:T(2,128)S(1)}, f32[12,2,128]{2,1,0:T(2,128)S(1)}, u32[]{:S(2)}, u32[]{:S(2)}) collective-permute-start(f32[12,2,128]{2,1,0:T(2,128)S(1)} %get-tuple-element.421), channel_id=1, source_target_pairs={{0,1},{1,2},{2,3},{3,0},{4,5},{5,6},{6,7},{7,4},{8,9},{9,10},{10,1... | collective-permute-start | bytes 36872 | tf_op jit(solution)/shard_map/ppermute | solution.py:20
  40.4 5.5 %collective-permute-start.4 = (f32[3,2,20,128]{3,2,1,0:T(8,128)S(1)}, f32[3,2,20,128]{3,2,1,0:T(8,128)S(1)}, u32[]{:S(2)}, u32[]{:S(2)}) collective-permute-start(f32[3,2,20,128]{3,2,1,0:T(8,128)S(1)} %get-tuple-element.280), channel_id=1, source_target_pairs={{0,4},{4,8},{8,12},{12,0},{1,5},{5,9},{9,13},{13,1},{2,6},{6,10},{... | collective-permute-start | bytes 184328 | tf_op jit(solution)/shard_map/ppermute | solution.py:20
  40.5 15.0 %collective-permute-start.13 = (f32[3,10,1,128]{3,2,1,0:T(1,128)S(1)}, f32[3,10,1,128]{3,2,1,0:T(1,128)S(1)}, u32[]{:S(2)}, u32[]{:S(2)}) collective-permute-start(f32[3,10,1,128]{3,2,1,0:T(1,128)S(1)} %get-tuple-element.317), channel_id=1, source_target_pairs={{1,0},{2,1},{3,2},{0,3},{5,4},{6,5},{7,6},{4,7},{9,8},{10,9},{11,1... | collective-permute-start | bytes 46088 | tf_op jit(solution)/shard_map/ppermute | solution.py:21
  40.6 14.9 %collective-permute-start.15 = (f32[3,10,1,128]{3,2,1,0:T(1,128)S(1)}, f32[3,10,1,128]{3,2,1,0:T(1,128)S(1)}, u32[]{:S(2)}, u32[]{:S(2)}) collective-permute-start(f32[3,10,1,128]{3,2,1,0:T(1,128)S(1)} %get-tuple-element.318), channel_id=1, source_target_pairs={{0,1},{1,2},{2,3},{3,0},{4,5},{5,6},{6,7},{7,4},{8,9},{9,10},{10,1... | collective-permute-start | bytes 46088 | tf_op jit(solution)/shard_map/ppermute | solution.py:20
  57.4 4.5 %collective-permute-start.17 = (f32[3,1,16,128]{3,2,1,0:T(8,128)S(1)}, f32[3,1,16,128]{3,2,1,0:T(8,128)S(1)}, u32[]{:S(2)}, u32[]{:S(2)}) collective-permute-start(f32[3,1,16,128]{3,2,1,0:T(8,128)S(1)} %get-tuple-element.413), channel_id=1, source_target_pairs={{0,4},{4,8},{8,12},{12,0},{1,5},{5,9},{9,13},{13,1},{2,6},{6,10},{... | collective-permute-start | bytes 73736 | tf_op jit(solution)/shard_map/ppermute | solution.py:20
  65.9 4.5 %collective-permute-start.21 = (f32[3,1,16,128]{3,2,1,0:T(8,128)S(1)}, f32[3,1,16,128]{3,2,1,0:T(8,128)S(1)}, u32[]{:S(2)}, u32[]{:S(2)}) collective-permute-start(f32[3,1,16,128]{3,2,1,0:T(8,128)S(1)} %get-tuple-element.407), channel_id=1, source_target_pairs={{0,4},{4,8},{8,12},{12,0},{1,5},{5,9},{9,13},{13,1},{2,6},{6,10},{... | collective-permute-start | bytes 73736 | tf_op jit(solution)/shard_map/ppermute | solution.py:20
  74.8 4.5 %collective-permute-start.25 = (f32[3,1,16,128]{3,2,1,0:T(8,128)S(1)}, f32[3,1,16,128]{3,2,1,0:T(8,128)S(1)}, u32[]{:S(2)}, u32[]{:S(2)}) collective-permute-start(f32[3,1,16,128]{3,2,1,0:T(8,128)S(1)} %get-tuple-element.401), channel_id=1, source_target_pairs={{0,4},{4,8},{8,12},{12,0},{1,5},{5,9},{9,13},{13,1},{2,6},{6,10},{... | collective-permute-start | bytes 73736 | tf_op jit(solution)/shard_map/ppermute | solution.py:20
  84.1 4.5 %collective-permute-start.29 = (f32[3,1,16,128]{3,2,1,0:T(8,128)S(1)}, f32[3,1,16,128]{3,2,1,0:T(8,128)S(1)}, u32[]{:S(2)}, u32[]{:S(2)}) collective-permute-start(f32[3,1,16,128]{3,2,1,0:T(8,128)S(1)} %get-tuple-element.395), channel_id=1, source_target_pairs={{0,4},{4,8},{8,12},{12,0},{1,5},{5,9},{9,13},{13,1},{2,6},{6,10},{... | collective-permute-start | bytes 73736 | tf_op jit(solution)/shard_map/ppermute | solution.py:20
  88.7 4.5 %collective-permute-start.30 = (f32[3,10,1,128]{3,2,1,0:T(1,128)S(1)}, f32[3,10,1,128]{3,2,1,0:T(1,128)S(1)}, u32[]{:S(2)}, u32[]{:S(2)}) collective-permute-start(f32[3,10,1,128]{3,2,1,0:T(1,128)S(1)} %get-tuple-element.309), channel_id=1, source_target_pairs={{1,0},{2,1},{3,2},{0,3},{5,4},{6,5},{7,6},{4,7},{9,8},{10,9},{11,1... | collective-permute-start | bytes 46088 | tf_op jit(solution)/shard_map/ppermute | solution.py:21
  93.5 4.5 %collective-permute-start.33 = (f32[3,1,16,128]{3,2,1,0:T(8,128)S(1)}, f32[3,1,16,128]{3,2,1,0:T(8,128)S(1)}, u32[]{:S(2)}, u32[]{:S(2)}) collective-permute-start(f32[3,1,16,128]{3,2,1,0:T(8,128)S(1)} %get-tuple-element.389), channel_id=1, source_target_pairs={{0,4},{4,8},{8,12},{12,0},{1,5},{5,9},{9,13},{13,1},{2,6},{6,10},{... | collective-permute-start | bytes 73736 | tf_op jit(solution)/shard_map/ppermute | solution.py:20
  102.9 4.5 %collective-permute-start.37 = (f32[3,1,16,128]{3,2,1,0:T(8,128)S(1)}, f32[3,1,16,128]{3,2,1,0:T(8,128)S(1)}, u32[]{:S(2)}, u32[]{:S(2)}) collective-permute-start(f32[3,1,16,128]{3,2,1,0:T(8,128)S(1)} %get-tuple-element.383), channel_id=1, source_target_pairs={{0,4},{4,8},{8,12},{12,0},{1,5},{5,9},{9,13},{13,1},{2,6},{6,10},{... | collective-permute-start | bytes 73736 | tf_op jit(solution)/shard_map/ppermute | solution.py:20
  112.2 4.6 %collective-permute-start.41 = (f32[3,1,16,128]{3,2,1,0:T(8,128)S(1)}, f32[3,1,16,128]{3,2,1,0:T(8,128)S(1)}, u32[]{:S(2)}, u32[]{:S(2)}) collective-permute-start(f32[3,1,16,128]{3,2,1,0:T(8,128)S(1)} %get-tuple-element.377), channel_id=1, source_target_pairs={{0,4},{4,8},{8,12},{12,0},{1,5},{5,9},{9,13},{13,1},{2,6},{6,10},{... | collective-permute-start | bytes 73736 | tf_op jit(solution)/shard_map/ppermute | solution.py:20
  121.5 4.6 %collective-permute-start.45 = (f32[3,1,16,128]{3,2,1,0:T(8,128)S(1)}, f32[3,1,16,128]{3,2,1,0:T(8,128)S(1)}, u32[]{:S(2)}, u32[]{:S(2)}) collective-permute-start(f32[3,1,16,128]{3,2,1,0:T(8,128)S(1)} %get-tuple-element.371), channel_id=1, source_target_pairs={{0,4},{4,8},{8,12},{12,0},{1,5},{5,9},{9,13},{13,1},{2,6},{6,10},{... | collective-permute-start | bytes 73736 | tf_op jit(solution)/shard_map/ppermute | solution.py:20
  130.9 4.6 %collective-permute-start.49 = (f32[3,1,16,128]{3,2,1,0:T(8,128)S(1)}, f32[3,1,16,128]{3,2,1,0:T(8,128)S(1)}, u32[]{:S(2)}, u32[]{:S(2)}) collective-permute-start(f32[3,1,16,128]{3,2,1,0:T(8,128)S(1)} %get-tuple-element.365), channel_id=1, source_target_pairs={{0,4},{4,8},{8,12},{12,0},{1,5},{5,9},{9,13},{13,1},{2,6},{6,10},{... | collective-permute-start | bytes 73736 | tf_op jit(solution)/shard_map/ppermute | solution.py:20
  135.6 4.5 %collective-permute-start.50 = (f32[3,10,1,128]{3,2,1,0:T(1,128)S(1)}, f32[3,10,1,128]{3,2,1,0:T(1,128)S(1)}, u32[]{:S(2)}, u32[]{:S(2)}) collective-permute-start(f32[3,10,1,128]{3,2,1,0:T(1,128)S(1)} %get-tuple-element.299), channel_id=1, source_target_pairs={{1,0},{2,1},{3,2},{0,3},{5,4},{6,5},{7,6},{4,7},{9,8},{10,9},{11,1... | collective-permute-start | bytes 46088 | tf_op jit(solution)/shard_map/ppermute | solution.py:21
  140.4 4.5 %collective-permute-start.53 = (f32[3,1,16,128]{3,2,1,0:T(8,128)S(1)}, f32[3,1,16,128]{3,2,1,0:T(8,128)S(1)}, u32[]{:S(2)}, u32[]{:S(2)}) collective-permute-start(f32[3,1,16,128]{3,2,1,0:T(8,128)S(1)} %get-tuple-element.359), channel_id=1, source_target_pairs={{0,4},{4,8},{8,12},{12,0},{1,5},{5,9},{9,13},{13,1},{2,6},{6,10},{... | collective-permute-start | bytes 73736 | tf_op jit(solution)/shard_map/ppermute | solution.py:20
  149.8 4.6 %collective-permute-start.57 = (f32[3,1,16,128]{3,2,1,0:T(8,128)S(1)}, f32[3,1,16,128]{3,2,1,0:T(8,128)S(1)}, u32[]{:S(2)}, u32[]{:S(2)}) collective-permute-start(f32[3,1,16,128]{3,2,1,0:T(8,128)S(1)} %get-tuple-element.353), channel_id=1, source_target_pairs={{0,4},{4,8},{8,12},{12,0},{1,5},{5,9},{9,13},{13,1},{2,6},{6,10},{... | collective-permute-start | bytes 73736 | tf_op jit(solution)/shard_map/ppermute | solution.py:20
  154.4 4.6 %collective-permute-start.58 = (f32[3,10,1,128]{3,2,1,0:T(1,128)S(1)}, f32[3,10,1,128]{3,2,1,0:T(1,128)S(1)}, u32[]{:S(2)}, u32[]{:S(2)}) collective-permute-start(f32[3,10,1,128]{3,2,1,0:T(1,128)S(1)} %get-tuple-element.295), channel_id=1, source_target_pairs={{1,0},{2,1},{3,2},{0,3},{5,4},{6,5},{7,6},{4,7},{9,8},{10,9},{11,1... | collective-permute-start | bytes 46088 | tf_op jit(solution)/shard_map/ppermute | solution.py:21
  159.3 4.6 %collective-permute-start.61 = (f32[3,1,16,128]{3,2,1,0:T(8,128)S(1)}, f32[3,1,16,128]{3,2,1,0:T(8,128)S(1)}, u32[]{:S(2)}, u32[]{:S(2)}) collective-permute-start(f32[3,1,16,128]{3,2,1,0:T(8,128)S(1)} %get-tuple-element.347), channel_id=1, source_target_pairs={{0,4},{4,8},{8,12},{12,0},{1,5},{5,9},{9,13},{13,1},{2,6},{6,10},{... | collective-permute-start | bytes 73736 | tf_op jit(solution)/shard_map/ppermute | solution.py:20
  168.6 4.6 %collective-permute-start.65 = (f32[3,1,16,128]{3,2,1,0:T(8,128)S(1)}, f32[3,1,16,128]{3,2,1,0:T(8,128)S(1)}, u32[]{:S(2)}, u32[]{:S(2)}) collective-permute-start(f32[3,1,16,128]{3,2,1,0:T(8,128)S(1)} %get-tuple-element.341), channel_id=1, source_target_pairs={{0,4},{4,8},{8,12},{12,0},{1,5},{5,9},{9,13},{13,1},{2,6},{6,10},{... | collective-permute-start | bytes 73736 | tf_op jit(solution)/shard_map/ppermute | solution.py:20
  177.9 4.6 %collective-permute-start.69 = (f32[3,1,16,128]{3,2,1,0:T(8,128)S(1)}, f32[3,1,16,128]{3,2,1,0:T(8,128)S(1)}, u32[]{:S(2)}, u32[]{:S(2)}) collective-permute-start(f32[3,1,16,128]{3,2,1,0:T(8,128)S(1)} %get-tuple-element.335), channel_id=1, source_target_pairs={{0,4},{4,8},{8,12},{12,0},{1,5},{5,9},{9,13},{13,1},{2,6},{6,10},{... | collective-permute-start | bytes 73736 | tf_op jit(solution)/shard_map/ppermute | solution.py:20
  187.4 4.6 %collective-permute-start.73 = (f32[3,1,16,128]{3,2,1,0:T(8,128)S(1)}, f32[3,1,16,128]{3,2,1,0:T(8,128)S(1)}, u32[]{:S(2)}, u32[]{:S(2)}) collective-permute-start(f32[3,1,16,128]{3,2,1,0:T(8,128)S(1)} %get-tuple-element.329), channel_id=1, source_target_pairs={{0,4},{4,8},{8,12},{12,0},{1,5},{5,9},{9,13},{13,1},{2,6},{6,10},{... | collective-permute-start | bytes 73736 | tf_op jit(solution)/shard_map/ppermute | solution.py:20
  196.8 4.9 %collective-permute-start.76 = (f32[3,2,16,128]{3,2,1,0:T(8,128)S(1)}, f32[3,2,16,128]{3,2,1,0:T(8,128)S(1)}, u32[]{:S(2)}, u32[]{:S(2)}) collective-permute-start(f32[3,2,16,128]{3,2,1,0:T(8,128)S(1)} %get-tuple-element.323), channel_id=1, source_target_pairs={{0,4},{4,8},{8,12},{12,0},{1,5},{5,9},{9,13},{13,1},{2,6},{6,10},{... | collective-permute-start | bytes 147464 | tf_op jit(solution)/shard_map/ppermute | solution.py:20
  196.8 4.8 %collective-permute-start.77 = (f32[3,2,16,128]{3,2,1,0:T(8,128)S(1)}, f32[3,2,16,128]{3,2,1,0:T(8,128)S(1)}, u32[]{:S(2)}, u32[]{:S(2)}) collective-permute-start(f32[3,2,16,128]{3,2,1,0:T(8,128)S(1)} %get-tuple-element.324), channel_id=1, source_target_pairs={{4,0},{8,4},{12,8},{0,12},{5,1},{9,5},{13,9},{1,13},{6,2},{10,6},{... | collective-permute-start | bytes 147464 | tf_op jit(solution)/shard_map/ppermute | solution.py:21
  221.2 4.7 %collective-permute-start.80 = (f32[1,3,2,3,128]{4,3,2,1,0:T(4,128)S(1)}, f32[1,3,2,3,128]{4,3,2,1,0:T(4,128)S(1)}, u32[]{:S(2)}, u32[]{:S(2)}) collective-permute-start(f32[1,3,2,3,128]{4,3,2,1,0:T(4,128)S(1)} %bitcast.174), channel_id=1, source_target_pairs={{0,4},{4,8},{8,12},{12,0},{1,5},{5,9},{9,13},{13,1},{2,6},{6,10},{... | collective-permute-start | bytes 27656 | tf_op jit(solution)/shard_map/ppermute | solution.py:20
  221.3 4.6 %collective-permute-start.81 = (f32[1,3,2,3,128]{4,3,2,1,0:T(4,128)S(1)}, f32[1,3,2,3,128]{4,3,2,1,0:T(4,128)S(1)}, u32[]{:S(2)}, u32[]{:S(2)}) collective-permute-start(f32[1,3,2,3,128]{4,3,2,1,0:T(4,128)S(1)} %bitcast.173), channel_id=1, source_target_pairs={{4,0},{8,4},{12,8},{0,12},{5,1},{9,5},{13,9},{1,13},{6,2},{10,6},{... | collective-permute-start | bytes 27656 | tf_op jit(solution)/shard_map/ppermute | solution.py:21
  (59 other events, 182.8 us)
where the time goes:
time: 231 us
  starting transfers between devices  98.8 us (43%)
  waiting for transfers between devices  89 us (39%)
  matrix products  20.8 us (9%)
  local copies, waits for them, and re-layouts  8.62 us (4%)
  other arithmetic  8.32 us (4%)
  loops' own time  3.69 us (2%)
    ppermute x42, starting transfers between devices, extended(): after = lax.ppermute(initial, axis, down)  53.8 us
    ppermute x42, waiting for transfers between devices, extended(): after = lax.ppermute(initial, axis, down)  47.4 us
    ppermute x42, starting transfers between devices, extended(): before = lax.ppermute(last, axis, up)  44.9 us
    ppermute x42, waiting for transfers between devices, extended(): before = lax.ppermute(last, axis, up)  41.6 us
    dot_general x18, matrix products, spread_block(): jnp.dot(left, table_z.T, precision=lax.Precision.HIGHEST, preferred_eleme...  11.2 us
    dot_general x18, matrix products, sample_block(): jnp.dot(field_rows, table_z, precision=lax.Precision.HIGHEST, preferred_e...  8.46 us
  transfers between devices with their start and end apart: 84, of which 58 were waited for; matrix products, arithmetic and copies ran while one was open for 8% of the time, Pallas kernels for 0%

commit v1 on v0

v1 whole, which is shorter than its diff:
```python
import functools

import jax
import jax.numpy as jnp
from jax import lax
from jax.experimental import pallas as pl
from jax.experimental.pallas import tpu as pltpu
from jax.sharding import PartitionSpec as P

SWEEPS = 8
MESH = pl.DeviceIdType.MESH
F32 = jnp.float32
BF16 = jnp.bfloat16
DIRS = [(dx, dy) for dx in (-1, 0, 1) for dy in (-1, 0, 1)]
SIDES = [d for d in range(9) if d != 4]
CORNERS = [0, 2, 6, 8]
YB = 24
R0 = 9
NT = (((1,), (1,)), ((), ()))


def split(value):
    scaled = value * 65537.0
    high = scaled - (scaled - value)
    return high.astype(BF16), (value - high).astype(BF16)


def spread_reach(step, last):
    if step == 0:
        return None
    if step > 0:
        return [(last, -1), (last + 1, 0), (last + 2, 1)]
    return [(-1, last), (0, last + 1)]


def flow_reach(step, last):
    if step > 0:
        return [(last, -1)]
    return [(0, last + 1), (1, last + 2)]


def spread_corner(d, nx, ny):
    dx, dy = DIRS[d]
    rows = []
    over_x = spread_reach(dx, nx - 1) or [(-1, -1), (nx, nx)]
    over_y = spread_reach(dy, ny - 1) or [(-1, -1), (ny, ny)]
    for sx, tx in over_x:
        for sy, ty in over_y:
            if not (tx in (-1, nx) and ty in (-1, ny)):
                rows.append((sx, sy, tx, ty))
    return rows


def flow_corner(d, nx, ny):
    dx, dy = DIRS[d]
    return [
        (sx, sy, tx, ty)
        for sx, tx in flow_reach(dx, nx - 1)
        for sy, ty in flow_reach(dy, ny - 1)
    ]


def kernel(
    size_x, size_y,
    vel, visc, force, weights, cells, count, dest,
    flow, mvel,
    S, V, C, inv, src, G, fld_hi, fld_lo, fld, packed,
    mk_tx, mk_rx, mk_s, mk_r,
    vx_rx, vy_tx, vy_rx, vc_tx, vc_rx, v_s, v_r,
    sx_tx, sx_rx, sy_tx, sy_rx, sc_tx, sc_rx, st_s, st_r,
    gxp_rx, gxm_rx, gyp_tx, gyp_rx, gym_tx, gym_rx, gc_tx, gc_rx, g_s, g_r,
    fxp_rx, fxm_rx, fyp_tx, fyp_rx, fym_tx, fym_rx, fc_tx, fc_rx, f_s, f_r,
    ret_tx, ret_rx, ret_s, ret_r,
):
    nx, ny, nz = visc.shape
    blocks, markers = force.shape[0], force.shape[2]
    here_x = lax.axis_index("gx")
    here_y = lax.axis_index("gy")

    def at(d, sign=1):
        dx, dy = DIRS[d]
        return {
            "gx": lax.rem(here_x + (sign * dx + size_x), size_x),
            "gy": lax.rem(here_y + (sign * dy + size_y), size_y),
        }

    def copy(a, b, s, r, d, sign=1):
        return pltpu.make_async_remote_copy(
            src_ref=a, dst_ref=b, send_sem=s, recv_sem=r,
            device_id=at(d, sign), device_id_type=MESH,
        )

    barrier = pltpu.get_barrier_semaphore()
    for d in SIDES:
        pl.semaphore_signal(barrier, inc=1, device_id=at(d), device_id_type=MESH)

    lane = lax.broadcasted_iota(jnp.int32, (1, markers), 1)
    for b in range(blocks):
        live = lane < count[b]
        packed[b, 0:3] = jnp.where(live, force[b], 0.0)
        for k in range(3):
            packed[b, 3 + 4 * k:7 + 4 * k] = jnp.where(live, weights[b, k], 0.0)
        packed[b, 15:18] = jnp.where(live, cells[b].astype(F32), 0.0)
        packed[b, 18:24] = jnp.zeros((6, markers), F32)
    going, rank = [], []
    for b in range(blocks):
        to = dest[b]
        step_x = lax.rem(lax.div(to, size_y) - here_x + (1 + size_x), size_x)
        step_y = lax.rem(lax.rem(to, size_y) - here_y + (1 + size_y), size_y)
        going.append(step_x * 3 + step_y)
        r = jnp.int32(0)
        for e in range(b):
            r = r + (going[e] == going[b]).astype(jnp.int32)
        rank.append(r)
    slot_of = [going[b] * 2 + rank[b] for b in range(blocks)]
    for d in range(9):
        for k in range(2):
            which, valid = jnp.int32(0), jnp.int32(0)
            for b in range(blocks):
                hit = (slot_of[b] == d * 2 + k).astype(jnp.int32)
                which, valid = which + b * hit, valid + hit
            block = packed[which] * valid.astype(F32)
            if d == 4:
                mk_rx[d, k] = block
            else:
                mk_tx[d, k] = block

    pl.semaphore_wait(barrier, 8)
    mk = {d: copy(mk_tx.at[d], mk_rx.at[d], mk_s.at[d], mk_r.at[d], d) for d in SIDES}
    for d in SIDES:
        mk[d].start()

    for i, lo in ((0, 0), (1, ny - 2)):
        for k in range(2):
            vy_tx[i, k] = visc[:, lo + k, :]
    for i, d in enumerate(CORNERS):
        dx, dy = DIRS[d]
        x, y = (nx - 1 if dx > 0 else 0), (ny - 1 if dy > 0 else 0)
        vc_tx[i] = visc[x, y:y + 1, :]
    vcopies = [
        copy(visc.at[0:2], vx_rx.at[0], v_s.at[1], v_r.at[1], 1),
        copy(visc.at[nx - 2:nx], vx_rx.at[1], v_s.at[7], v_r.at[7], 7),
        copy(vy_tx.at[0], vy_rx.at[0], v_s.at[3], v_r.at[3], 3),
        copy(vy_tx.at[1], vy_rx.at[1], v_s.at[5], v_r.at[5], 5),
    ] + [
        copy(vc_tx.at[i], vc_rx.at[i], v_s.at[d], v_r.at[d], d) for i, d in enumerate(CORNERS)
    ]
    for c in vcopies:
        c.start()

    S[...] = jnp.zeros(S.shape, F32)
    V[...] = jnp.zeros(V.shape, F32)
    for c in range(3):
        S[c, 2:2 + nx, R0:R0 + ny, :] = vel[c]
    odd = (
        lax.broadcasted_iota(jnp.int32, (ny, nz), 0) + lax.broadcasted_iota(jnp.int32, (ny, nz), 1)
    ) % 2 == 1
    odd_x = (
        lax.broadcasted_iota(jnp.int32, (nx, nz), 0) + lax.broadcasted_iota(jnp.int32, (nx, nz), 1)
    ) % 2 == 1

    def state_copies(slot):
        out = [
            copy(sx_tx.at[slot, i], sx_rx.at[slot, i], st_s.at[slot, d], st_r.at[slot, d], d)
            for i, d in ((0, 1), (1, 7))
        ]
        out += [
            copy(sy_tx.at[slot, i], sy_rx.at[slot, i], st_s.at[slot, d], st_r.at[slot, d], d)
            for i, d in ((0, 3), (1, 5))
        ]
        out += [
            copy(sc_tx.at[slot, i], sc_rx.at[slot, i], st_s.at[slot, d], st_r.at[slot, d], d)
            for i, d in enumerate(CORNERS)
        ]
        return out

    def send_state(slot):
        for c in range(3):
            for i, x in ((0, 0), (1, nx - 2)):
                sx_tx[slot, i, c] = jnp.where(
                    odd, S[c, 2 + x, R0:R0 + ny, :], S[c, 3 + x, R0:R0 + ny, :]
                )
            for i, y in ((0, 0), (1, ny - 2)):
                sy_tx[slot, i, c] = jnp.where(
                    odd_x, S[c, 2:2 + nx, R0 + y, :], S[c, 2:2 + nx, R0 + y + 1, :]
                )
            for i, d in enumerate(CORNERS):
                dx, dy = DIRS[d]
                x, y = (nx - 1 if dx > 0 else 0), (ny - 1 if dy > 0 else 0)
                sc_tx[slot, i, c] = S[c, 2 + x, R0 + y:R0 + y + 1, :]
        for c in state_copies(slot):
            c.start()

    def take_state(slot):
        for c in state_copies(slot):
            c.wait()
        for c in range(3):
            for i, x in ((0, nx), (1, -2)):
                plane = sx_rx[slot, i, c]
                S[c, 2 + x, R0:R0 + ny, :] = plane
                S[c, 3 + x, R0:R0 + ny, :] = plane
            for i, y in ((0, ny), (1, -2)):
                tile = sy_rx[slot, i, c]
                S[c, 2:2 + nx, R0 + y, :] = tile
                S[c, 2:2 + nx, R0 + y + 1, :] = tile
            for i, d in enumerate(CORNERS):
                dx, dy = DIRS[d]
                x, y = (-1 if dx > 0 else nx), (-1 if dy > 0 else ny)
                S[c, 2 + x, R0 + y:R0 + y + 1, :] = sc_rx[slot, i, c]

    send_state(0)

    V[2:2 + nx, R0:R0 + ny, :] = visc[...]
    for c in vcopies:
        c.wait()
    for i, x in ((0, nx), (1, -2)):
        V[2 + x:4 + x, R0:R0 + ny, :] = vx_rx[i]
    for i, y in ((0, ny), (1, -2)):
        for k in range(2):
            V[2:2 + nx, R0 + y + k, :] = vy_rx[i, k]
    for i, d in enumerate(CORNERS):
        dx, dy = DIRS[d]
        x, y = (-1 if dx > 0 else nx), (-1 if dy > 0 else ny)
        V[2 + x, R0 + y:R0 + y + 1, :] = vc_rx[i]
    lo, hi = R0 - 1, R0 - 1 + 24

    def coefficient(i, carry):
        mid = V[i + 1, lo:hi, :]
        around = [
            V[i + 2, lo:hi, :],
            V[i, lo:hi, :],
            V[i + 1, lo + 1:hi + 1, :],
            V[i + 1, lo - 1:hi - 1, :],
            pltpu.roll(mid, nz - 1, 1),
            pltpu.roll(mid, 1, 1),
        ]
        faces = [mid + a for a in around]
        total = faces[0]
        for f in faces[1:]:
            total = total + f
        recip = 1.0 / (1.0 + total)
        inv[i] = recip
        for k in range(6):
            C[k, i] = faces[k] * recip
        return carry

    lax.fori_loop(0, nx + 2, coefficient, 0)

    row_x = lax.broadcasted_iota(jnp.int32, (16, markers), 0)
    row_y = lax.broadcasted_iota(jnp.int32, (YB, markers), 0)
    row_z = lax.broadcasted_iota(jnp.int32, (nz, markers), 0)

    def tables(blk):
        place = blk[15:18].astype(jnp.int32)
        tx = jnp.zeros((16, markers), F32)
        ty = jnp.zeros((YB, markers), F32)
        tz = jnp.zeros((nz, markers), F32)
        for o in range(4):
            px = place[0:1] + o
            py = place[1:2] + (o - 1)
            py = jnp.where(py < 0, py + YB, py)
            pz = (place[2:3] + (o - 1 + nz)) % nz
            tx = jnp.where(row_x == px, blk[3 + o:4 + o], tx)
            ty = jnp.where(row_y == py, blk[7 + o:8 + o], ty)
            tz = jnp.where(row_z == pz, blk[11 + o:12 + o], tz)
        txy = jnp.concatenate([tx[i:i + 1] * ty for i in range(nx + 4)], axis=0)
        return txy, tz

    G[...] = jnp.zeros(G.shape, F32)
    for c in range(3):
        G[1:1 + nx, 0:ny, c * nz:(c + 1) * nz] = vel[c]
    for d in SIDES:
        mk[d].wait()

    def dot(a, b, dims):
        return lax.dot_general(a, b, dims, preferred_element_type=F32)

    def spread(d, carry):
        left, right = [], []
        for k in range(2):
            blk = mk_rx[d, k]
            txy, tz = tables(blk)
            left.append(txy)
            right.append(jnp.concatenate([tz * blk[c:c + 1] for c in range(3)], axis=0))
        left_hi, left_lo = split(jnp.concatenate(left, axis=1))
        right_hi, right_lo = split(jnp.concatenate(right, axis=1))
        got = dot(left_hi, right_hi, NT) + dot(left_hi, right_lo, NT) + dot(left_lo, right_hi, NT)
        G[...] += got.reshape(G.shape)
        return carry

    lax.fori_loop(0, 9, spread, 0)

    def g_row(y):
        return y % YB

    for k, (y, _) in enumerate(spread_reach(1, ny - 1)):
        gyp_tx[k] = G[1:1 + nx, g_row(y), :]
    for k, (y, _) in enumerate(spread_reach(-1, ny - 1)):
        gym_tx[k] = G[1:1 + nx, g_row(y), :]
    for i, d in enumerate(SIDES):
        for k, (sx, sy, _, _) in enumerate(spread_corner(d, nx, ny)):
            gc_tx[i, k] = G[sx + 1, g_row(sy):g_row(sy) + 1, :]
    gcopies = [
        copy(G.at[nx:nx + 3, 0:ny], gxp_rx, g_s.at[7], g_r.at[7], 7),
        copy(G.at[0:2, 0:ny], gxm_rx, g_s.at[1], g_r.at[1], 1),
        copy(gyp_tx, gyp_rx, g_s.at[5], g_r.at[5], 5),
        copy(gym_tx, gym_rx, g_s.at[3], g_r.at[3], 3),
    ]
    for i, d in enumerate(SIDES):
        n = len(spread_corner(d, nx, ny))
        gcopies.append(copy(gc_tx.at[i, 0:n], gc_rx.at[i, 0:n], g_s.at[9 + i], g_r.at[9 + i], d))
    for c in gcopies:
        c.start()
    src[...] = jnp.zeros(src.shape, F32)
    for c in range(3):
        z = slice(c * nz, (c + 1) * nz)
        src[c, :, 1:2 + ny, :] = G[0:nx + 2, 0:ny + 1, z]
        src[c, :, 0:1, :] = G[0:nx + 2, YB - 1:YB, z]
    for c in gcopies:
        c.wait()
    for c in range(3):
        z = slice(c * nz, (c + 1) * nz)
        src[c, 0:3, 1:1 + ny, :] += gxp_rx[:, :, z]
        src[c, nx:nx + 2, 1:1 + ny, :] += gxm_rx[:, :, z]
        for k, (_, y) in enumerate(spread_reach(1, ny - 1)):
            src[c, 1:1 + nx, 1 + y, :] += gyp_rx[k, :, z]
        for k, (_, y) in enumerate(spread_reach(-1, ny - 1)):
            src[c, 1:1 + nx, 1 + y, :] += gym_rx[k, :, z]
        for i, d in enumerate(SIDES):
            for k, (_, _, x, y) in enumerate(spread_corner(d, nx, ny)):
                src[c, 1 + x, 1 + y:2 + y, :] += gc_rx[i, k, :, z]
        src[c] = src[c] * inv[...]

    def update(first, last, low, high, colour):
        rows = high - low
        parity = (
            lax.broadcasted_iota(jnp.int32, (rows, nz), 0)
            + lax.broadcasted_iota(jnp.int32, (rows, nz), 1)
            + low
        ) % 2
        a, b = R0 + low, R0 + high
        p, q = 1 + low, 1 + high
        for x in range(first, last):
            chosen = parity == (colour + x) % 2
            coef = [C[k, x + 1, p:q, :] for k in range(6)]
            for c in range(3):
                mid = S[c, x + 2, a:b, :]
                new = (
                    src[c, x + 1, p:q, :]
                    + coef[0] * S[c, x + 3, a:b, :]
                    + coef[1] * S[c, x + 1, a:b, :]
                    + coef[2] * S[c, x + 2, a + 1:b + 1, :]
                    + coef[3] * S[c, x + 2, a - 1:b - 1, :]
                    + coef[4] * pltpu.roll(mid, nz - 1, 1)
                    + coef[5] * pltpu.roll(mid, 1, 1)
                )
                S[c, x + 2, a:b, :] = jnp.where(chosen, new, mid)

    def sweep(r, carry):
        take_state(lax.rem(r, 2))
        update(-1, nx + 1, -1, 23, 0)
        update(0, nx, 0, ny, 1)

        @pl.when(r < SWEEPS - 1)
        def _():
            send_state(lax.rem(r + 1, 2))

        return carry

    lax.fori_loop(0, SWEEPS, sweep, 0)

    for c in range(3):
        flow[c] = S[c, 2:2 + nx, R0:R0 + ny, :]
        for k, (y, _) in enumerate(flow_reach(1, ny - 1)):
            fyp_tx[k, c] = S[c, 2:2 + nx, R0 + y, :]
        for k, (y, _) in enumerate(flow_reach(-1, ny - 1)):
            fym_tx[k, c] = S[c, 2:2 + nx, R0 + y, :]
        for i, d in enumerate(CORNERS):
            for k, (sx, sy, _, _) in enumerate(flow_corner(d, nx, ny)):
                fc_tx[i, 3 * k + c] = S[c, 2 + sx, R0 + sy:R0 + sy + 1, :]
    fcopies = [
        copy(flow.at[:, nx - 1:nx], fxp_rx, f_s.at[7], f_r.at[7], 7),
        copy(flow.at[:, 0:2], fxm_rx, f_s.at[1], f_r.at[1], 1),
        copy(fyp_tx, fyp_rx, f_s.at[5], f_r.at[5], 5),
        copy(fym_tx, fym_rx, f_s.at[3], f_r.at[3], 3),
    ]
    for i, d in enumerate(CORNERS):
        n = 3 * len(flow_corner(d, nx, ny))
        fcopies.append(copy(fc_tx.at[i, 0:n], fc_rx.at[i, 0:n], f_s.at[d], f_r.at[d], d))
    for c in fcopies:
        c.start()
    fld[...] = jnp.zeros(fld.shape, F32)
    for c in range(3):
        fld[c, 1:1 + nx, 0:ny, :] = S[c, 2:2 + nx, R0:R0 + ny, :]
    for c in fcopies:
        c.wait()
    fld[:, 0:1, 0:ny, :] = fxp_rx[...]
    fld[:, 1 + nx:3 + nx, 0:ny, :] = fxm_rx[...]
    for c in range(3):
        for k, (_, y) in enumerate(flow_reach(1, ny - 1)):
            fld[c, 1:1 + nx, g_row(y), :] = fyp_rx[k, c]
        for k, (_, y) in enumerate(flow_reach(-1, ny - 1)):
            fld[c, 1:1 + nx, g_row(y), :] = fym_rx[k, c]
        for i, d in enumerate(CORNERS):
            for k, (_, _, x, y) in enumerate(flow_corner(d, nx, ny)):
                fld[c, 1 + x, g_row(y):g_row(y) + 1, :] = fc_rx[i, 3 * k + c]
    high, low = split(fld[...].reshape(-1, nz))
    fld_hi[...] = high
    fld_lo[...] = low
    NN = (((1,), (0,)), ((), ()))

    def sample(d, carry):
        pairs = [tables(mk_rx[d, k]) for k in range(2)]
        txy = jnp.concatenate([p[0] for p in pairs], axis=1)
        tz_hi, tz_lo = split(jnp.concatenate([p[1] for p in pairs], axis=1))
        picked = dot(fld_hi[...], tz_hi, NN) + dot(fld_lo[...], tz_hi, NN) + dot(fld_hi[...], tz_lo, NN)
        rows = txy.shape[0]
        for c in range(3):
            total = jnp.sum(picked[c * rows:(c + 1) * rows] * txy, axis=0, keepdims=True)
            ret_tx[d, 0, c:c + 1] = total[:, :markers]
            ret_tx[d, 1, c:c + 1] = total[:, markers:]
        return carry

    ret_tx[...] = jnp.zeros(ret_tx.shape, F32)
    lax.fori_loop(0, 9, sample, 0)
    back = [copy(ret_tx.at[d], ret_rx.at[d], ret_s.at[d], ret_r.at[d], d, -1) for d in SIDES]
    for c in back:
        c.start()
    ret_rx[4] = ret_tx[4]
    for c in back:
        c.wait()
    for b in range(blocks):
        mvel[b] = ret_rx[jnp.clip(going[b], 0, 8), jnp.clip(rank[b], 0, 1)][0:3]


def local(velocity, viscosity, marker_force, delta_weights, marker_cells, block_count, destination):
    nx, ny, nz = viscosity.shape
    size_x, size_y = lax.axis_size("gx"), lax.axis_size("gy")
    blocks, _, markers = marker_force.shape
    dma = pltpu.SemaphoreType.DMA
    vmem = pltpu.VMEM
    rows = 3 * (nx + 4) * YB
    scratch = [
        vmem((3, nx + 4, 40, nz), F32),
        vmem((nx + 4, 40, nz), F32),
        vmem((6, nx + 2, 24, nz), F32),
        vmem((nx + 2, 24, nz), F32),
        vmem((3, nx + 2, 24, nz), F32),
        vmem((nx + 4, YB, 3 * nz), F32),
        vmem((rows, nz), BF16),
        vmem((rows, nz), BF16),
        vmem((3, nx + 4, YB, nz), F32),
        vmem((blocks, 24, markers), F32),
        vmem((9, 2, 24, markers), F32), vmem((9, 2, 24, markers), F32), dma((9,)), dma((9,)),
        vmem((2, 2, ny, nz), F32),
        vmem((2, 2, nx, nz), F32), vmem((2, 2, nx, nz), F32),
        vmem((4, 1, nz), F32), vmem((4, 1, nz), F32), dma((9,)), dma((9,)),
        vmem((2, 2, 3, ny, nz), F32), vmem((2, 2, 3, ny, nz), F32),
        vmem((2, 2, 3, nx, nz), F32), vmem((2, 2, 3, nx, nz), F32),
        vmem((2, 4, 3, 1, nz), F32), vmem((2, 4, 3, 1, nz), F32), dma((2, 9)), dma((2, 9)),
        vmem((3, ny, 3 * nz), F32), vmem((2, ny, 3 * nz), F32),
        vmem((3, nx, 3 * nz), F32), vmem((3, nx, 3 * nz), F32),
        vmem((2, nx, 3 * nz), F32), vmem((2, nx, 3 * nz), F32),
        vmem((8, 8, 1, 3 * nz), F32), vmem((8, 8, 1, 3 * nz), F32), dma((17,)), dma((17,)),
        vmem((3, 1, ny, nz), F32), vmem((3, 2, ny, nz), F32),
        vmem((1, 3, nx, nz), F32), vmem((1, 3, nx, nz), F32),
        vmem((2, 3, nx, nz), F32), vmem((2, 3, nx, nz), F32),
        vmem((4, 12, 1, nz), F32), vmem((4, 12, 1, nz), F32), dma((9,)), dma((9,)),
        vmem((9, 2, 8, markers), F32), vmem((9, 2, 8, markers), F32), dma((9,)), dma((9,)),
    ]
    in_vmem = pl.BlockSpec(memory_space=pltpu.VMEM)
    in_smem = pl.BlockSpec(memory_space=pltpu.SMEM)
    return pl.pallas_call(
        functools.partial(kernel, size_x, size_y),
        out_shape=(
            jax.ShapeDtypeStruct(velocity.shape, F32),
            jax.ShapeDtypeStruct(marker_force.shape, F32),
        ),
        in_specs=[in_vmem] * 5 + [in_smem] * 2,
        out_specs=(in_vmem, in_vmem),
        scratch_shapes=scratch,
        compiler_params=pltpu.CompilerParams(
            collective_id=0, has_side_effects=True, vmem_limit_bytes=40 * 1024 * 1024
        ),
    )(velocity, viscosity, marker_force, delta_weights, marker_cells, block_count, destination)


def solution(mesh):
    return jax.shard_map(
        local,
        mesh=mesh,
        in_specs=(
            P(None, ("groups", "gx"), "gy", None),
            P(("groups", "gx"), "gy", None),
            P(("groups", "gx", "gy"), None, None),
            P(("groups", "gx", "gy"), None, None, None),
            P(("groups", "gx", "gy"), None, None),
            P(("groups", "gx", "gy")),
            P(("groups", "gx", "gy")),
        ),
        out_specs=(P(None, ("groups", "gx"), "gy", None), P(("groups", "gx", "gy"), None, None)),
        check_vma=False,
    )
```

time: 231 us -> 78 us (0.34)
  starting transfers between devices: 98.8 us -> 0 us
  waiting for transfers between devices: 89 us -> 0 us
  Pallas kernels: 0 us -> 72.4 us
  matrix products: 20.8 us -> 0 us
  other arithmetic: 8.32 us -> 0 us
  local copies, waits for them, and re-layouts: 8.62 us -> 4.51 us
  loops' own time: 3.69 us -> 0 us
    ppermute x84 -> x0, starting transfers between devices: 98.8 us -> none  [the longest x42 53.8 us: extended(): after = lax.ppermute(initial, axis, down)]
    ppermute x84 -> x0, waiting for transfers between devices: 89 us -> none  [the longest x42 47.4 us: extended(): after = lax.ppermute(initial, axis, down)]
    pallas_call x0 -> x1, Pallas kernels: none -> 72.4 us  [local(): pl.pallas_call(functools.partial(kernel, size_x, size_y), out_shape=(jax....]
    dot_general x38 -> x0, matrix products: 20.8 us -> none  [the longest x18 11.2 us: spread_block(): jnp.dot(left, table_z.T, precision=lax.Precision.HIGHEST, preferred_eleme...]
    select_n x52 -> x0, other arithmetic: 4.15 us -> none  [the longest x16 3.64 us: relax_cells(): return jnp.where(chosen, (source_term + KAPPA * summed) / diagonal, centre)]
    slice x66 -> x0, local copies, waits for them, and re-layouts: 3.92 us -> none  [the longest x32 3.44 us: relax_cells(): jnp.roll(centre, 1, 3)]
    another operation x2 -> x0, loops' own time: 3.69 us -> none  [the longest x1 1.98 us: local(): lax.scan(spread_block, spread_init, (slot_force, slot_weights, slot_cells))]
  transfers between devices with their start and end apart: 84 -> 0, of which waited for: 58 -> 0; matrix products, arithmetic and copies ran while one was open for 8% -> 0% of each run, Pallas kernels for 0% -> 0%
where the time goes in v1:
time: 78 us; the launch traced here: 77.6 us
  Pallas kernels  72.4 us (93%)
  local copies, waits for them, and re-layouts  4.51 us (6%)
    pallas_call x1, Pallas kernels, local(): pl.pallas_call(functools.partial(kernel, size_x, size_y), out_shape=(jax....  72.4 us
    unnamed x13, local copies, waits for them, and re-layouts  3.91 us

profile of v1, /device:TPU:1, one launch (start us, length us, event | category | flops | bytes accessed | tf_op | source)
XLA Modules:
  0.0 77.6 jit_solution(4959556265320847267)
XLA Ops:
  0.6 0.0 copy-start.2
  0.6 0.7 copy.9.force
  1.4 0.0 copy-start.3
  1.4 0.0 copy-start.4
  1.4 0.7 copy.10.cells
  2.1 0.0 copy-done.2
  2.1 0.0 copy-done.3
  2.1 0.0 copy-done.4
  2.1 0.0 copy-start
  2.1 0.9 %copy-done = f32[3,8,16,128]{3,2,1,0:T(8,128)S(1)} copy-done((f32[3,8,16,128]{3,2,1,0:T(8,128)S(1)}, f32[3,8,16,128]{3,2,1,0:T(8,128)}, u32[]{:S(2)}) %copy-start) | copy-done | bytes 196632
  3.1 0.0 copy-start.1
  3.1 0.8 %copy-done.1 = f32[8,16,128]{2,1,0:T(8,128)S(1)} copy-done((f32[8,16,128]{2,1,0:T(8,128)S(1)}, f32[8,16,128]{2,1,0:T(8,128)}, u32[]{:S(2)}) %copy-start.1) | copy-done | bytes 65560
  3.9 72.4 %shard_map.86 = (f32[3,8,16,128]{3,2,1,0:T(8,128)S(1)}, f32[8,3,128]{2,1,0:T(4,128)S(1)}) custom-call(f32[3,8,16,128]{3,2,1,0:T(8,128)S(1)} %copy-done, f32[8,16,128]{2,1,0:T(8,128)S(1)} %copy-done.1, f32[8,3,128]{2,1,0:T(4,128)S(1)} %copy.9.force, f32[8,3,4,128]{3,2,1,0:T(4,128)S(1)} %copy-done.2, s32[8,3,128]{2,1,0:T(4,128)S(1)} %copy.10.cells, ...), custom_call_target="tpu_custom_call" | custom-call | tf_op jit(solution)/shard_map/pallas_call | solution.py:473
  76.3 0.6 copy.11
  77.0 0.7 copy.13
Async XLA Ops:
  0.6 1.5 %copy-start.2 = (f32[8,3,4,128]{3,2,1,0:T(4,128)S(1)}, f32[8,3,4,128]{3,2,1,0:T(4,128)}, u32[]{:S(2)}) copy-start(f32[8,3,4,128]{3,2,1,0:T(4,128)} %weights.1) | copy-start | bytes 147460
  1.4 0.7 copy-start.3
  1.4 0.8 copy-start.4
  2.1 0.9 %copy-start = (f32[3,8,16,128]{3,2,1,0:T(8,128)S(1)}, f32[3,8,16,128]{3,2,1,0:T(8,128)}, u32[]{:S(2)}) copy-start(f32[3,8,16,128]{3,2,1,0:T(8,128)} %vel.1) | copy-start | bytes 589828
  3.1 0.8 %copy-start.1 = (f32[8,16,128]{2,1,0:T(8,128)S(1)}, f32[8,16,128]{2,1,0:T(8,128)}, u32[]{:S(2)}) copy-start(f32[8,16,128]{2,1,0:T(8,128)} %visc.1) | copy-start | bytes 196612

commit v2 on v1

--- a/solution.py
+++ b/solution.py
@@ -78,7 +78,7 @@
     here_y = lax.axis_index("gy")
 
     def at(d, sign=1):
-        dx, dy = DIRS[d]
+        dx, dy = DIRS[d] if isinstance(d, int) else (d // 3 - 1, d % 3 - 1)
         return {
             "gx": lax.rem(here_x + (sign * dx + size_x), size_x),
             "gy": lax.rem(here_y + (sign * dy + size_y), size_y),
@@ -149,7 +149,6 @@
         c.start()
 
     S[...] = jnp.zeros(S.shape, F32)
-    V[...] = jnp.zeros(V.shape, F32)
     for c in range(3):
         S[c, 2:2 + nx, R0:R0 + ny, :] = vel[c]
     odd = (
@@ -159,57 +158,140 @@
         lax.broadcasted_iota(jnp.int32, (nx, nz), 0) + lax.broadcasted_iota(jnp.int32, (nx, nz), 1)
     ) % 2 == 1
 
-    def state_copies(slot):
-        out = [
+    def corner_cell(d):
+        dx, dy = DIRS[d]
+        return (nx - 1 if dx > 0 else 0), (ny - 1 if dy > 0 else 0)
+
+    def copies_x(slot):
+        return [
             copy(sx_tx.at[slot, i], sx_rx.at[slot, i], st_s.at[slot, d], st_r.at[slot, d], d)
             for i, d in ((0, 1), (1, 7))
+        ] + [
+            copy(sc_tx.at[slot, i], sc_rx.at[slot, i], st_s.at[slot, d], st_r.at[slot, d], d)
+            for i, d in enumerate(CORNERS)
         ]
-        out += [
+
+    def copies_y(slot):
+        return [
             copy(sy_tx.at[slot, i], sy_rx.at[slot, i], st_s.at[slot, d], st_r.at[slot, d], d)
             for i, d in ((0, 3), (1, 5))
         ]
-        out += [
-            copy(sc_tx.at[slot, i], sc_rx.at[slot, i], st_s.at[slot, d], st_r.at[slot, d], d)
-            for i, d in enumerate(CORNERS)
-        ]
-        return out
-
-    def send_state(slot):
-        for c in range(3):
-            for i, x in ((0, 0), (1, nx - 2)):
+
+    def send_x(slot):
+        sends = copies_x(slot)
+        for i, x in ((0, 0), (1, nx - 2)):
+            for c in range(3):
                 sx_tx[slot, i, c] = jnp.where(
                     odd, S[c, 2 + x, R0:R0 + ny, :], S[c, 3 + x, R0:R0 + ny, :]
                 )
-            for i, y in ((0, 0), (1, ny - 2)):
+            sends[i].start()
+        for i, d in enumerate(CORNERS):
+            x, y = corner_cell(d)
+            for c in range(3):
+                sc_tx[slot, i, c] = S[c, 2 + x, R0 + y:R0 + y + 1, :]
+            sends[2 + i].start()
+
+    def send_y(slot):
+        sends = copies_y(slot)
+        for i, y in ((0, 0), (1, ny - 2)):
+            for c in range(3):
                 sy_tx[slot, i, c] = jnp.where(
                     odd_x, S[c, 2:2 + nx, R0 + y, :], S[c, 2:2 + nx, R0 + y + 1, :]
                 )
-            for i, d in enumerate(CORNERS):
-                dx, dy = DIRS[d]
-                x, y = (nx - 1 if dx > 0 else 0), (ny - 1 if dy > 0 else 0)
-                sc_tx[slot, i, c] = S[c, 2 + x, R0 + y:R0 + y + 1, :]
-        for c in state_copies(slot):
-            c.start()
-
-    def take_state(slot):
-        for c in state_copies(slot):
+            sends[i].start()
+
+    def take_y(slot):
+        for c in copies_y(slot):
+            c.wait()
+        for c in range(3):
+            for i, y in ((0, ny), (1, -2)):
+                tile = sy_rx[slot, i, c]
+                S[c, 2:2 + nx, R0 + y, :] = tile
+                S[c, 2:2 + nx, R0 + y + 1, :] = tile
+
+    def take_x(slot):
+        for c in copies_x(slot):
             c.wait()
         for c in range(3):
             for i, x in ((0, nx), (1, -2)):
                 plane = sx_rx[slot, i, c]
                 S[c, 2 + x, R0:R0 + ny, :] = plane
                 S[c, 3 + x, R0:R0 + ny, :] = plane
-            for i, y in ((0, ny), (1, -2)):
-                tile = sy_rx[slot, i, c]
-                S[c, 2:2 + nx, R0 + y, :] = tile
-                S[c, 2:2 + nx, R0 + y + 1, :] = tile
             for i, d in enumerate(CORNERS):
                 dx, dy = DIRS[d]
                 x, y = (-1 if dx > 0 else nx), (-1 if dy > 0 else ny)
                 S[c, 2 + x, R0 + y:R0 + y + 1, :] = sc_rx[slot, i, c]
 
-    send_state(0)
-
+    send_x(0)
+    send_y(0)
+
+    row_x = lax.broadcasted_iota(jnp.int32, (16, markers), 0)
+    row_y = lax.broadcasted_iota(jnp.int32, (YB, markers), 0)
+    row_z = lax.broadcasted_iota(jnp.int32, (nz, markers), 0)
+
+    def tables(blk):
+        place = blk[15:18].astype(jnp.int32)
+        tx = jnp.zeros((16, markers), F32)
+        ty = jnp.zeros((YB, markers), F32)
+        tz = jnp.zeros((nz, markers), F32)
+        for o in range(4):
+            px = place[0:1] + o
+            py = place[1:2] + (o - 1)
+            py = jnp.where(py < 0, py + YB, py)
+            pz = (place[2:3] + (o - 1 + nz)) % nz
+            tx = jnp.where(row_x == px, blk[3 + o:4 + o], tx)
+            ty = jnp.where(row_y == py, blk[7 + o:8 + o], ty)
+            tz = jnp.where(row_z == pz, blk[11 + o:12 + o], tz)
+        txy = jnp.concatenate([tx[i:i + 1] * ty for i in range(nx + 4)], axis=0)
+        return txy, tz
+
+    G[...] = jnp.zeros(G.shape, F32)
+    for c in range(3):
+        G[1:1 + nx, 0:ny, c * nz:(c + 1) * nz] = vel[c]
+    def dot(a, b, dims):
+        return lax.dot_general(a, b, dims, preferred_element_type=F32)
+
+    def spread(d, carry):
+        left, right = [], []
+        for k in range(2):
+            blk = mk_rx[d, k]
+            txy, tz = tables(blk)
+            left.append(txy)
+            right.append(jnp.concatenate([tz * blk[c:c + 1] for c in range(3)], axis=0))
+        left_hi, left_lo = split(jnp.concatenate(left, axis=1))
+        right_hi, right_lo = split(jnp.concatenate(right, axis=1))
+        got = dot(left_hi, right_hi, NT) + dot(left_hi, right_lo, NT) + dot(left_lo, right_hi, NT)
+        G[...] += got.reshape(G.shape)
+        return carry
+
+    lax.fori_loop(4, 5, spread, 0)
+    for d in SIDES:
+        mk[d].wait()
+    lax.fori_loop(0, 4, spread, 0)
+    lax.fori_loop(5, 9, spread, 0)
+
+    def g_row(y):
+        return y % YB
+
+    for k, (y, _) in enumerate(spread_reach(1, ny - 1)):
+        gyp_tx[k] = G[1:1 + nx, g_row(y), :]
+    for k, (y, _) in enumerate(spread_reach(-1, ny - 1)):
+        gym_tx[k] = G[1:1 + nx, g_row(y), :]
+    for i, d in enumerate(SIDES):
+        for k, (sx, sy, _, _) in enumerate(spread_corner(d, nx, ny)):
+            gc_tx[i, k] = G[sx + 1, g_row(sy):g_row(sy) + 1, :]
+    gcopies = [
+        copy(G.at[nx:nx + 3, 0:ny], gxp_rx, g_s.at[7], g_r.at[7], 7),
+        copy(G.at[0:2, 0:ny], gxm_rx, g_s.at[1], g_r.at[1], 1),
+        copy(gyp_tx, gyp_rx, g_s.at[5], g_r.at[5], 5),
+        copy(gym_tx, gym_rx, g_s.at[3], g_r.at[3], 3),
+    ]
+    for i, d in enumerate(SIDES):
+        n = len(spread_corner(d, nx, ny))
+        gcopies.append(copy(gc_tx.at[i, 0:n], gc_rx.at[i, 0:n], g_s.at[9 + i], g_r.at[9 + i], d))
+    for c in gcopies:
+        c.start()
+    V[...] = jnp.zeros(V.shape, F32)
     V[2:2 + nx, R0:R0 + ny, :] = visc[...]
     for c in vcopies:
         c.wait()
@@ -246,71 +328,6 @@
 
     lax.fori_loop(0, nx + 2, coefficient, 0)
 
-    row_x = lax.broadcasted_iota(jnp.int32, (16, markers), 0)
-    row_y = lax.broadcasted_iota(jnp.int32, (YB, markers), 0)
-    row_z = lax.broadcasted_iota(jnp.int32, (nz, markers), 0)
-
-    def tables(blk):
-        place = blk[15:18].astype(jnp.int32)
-        tx = jnp.zeros((16, markers), F32)
-        ty = jnp.zeros((YB, markers), F32)
-        tz = jnp.zeros((nz, markers), F32)
-        for o in range(4):
-            px = place[0:1] + o
-            py = place[1:2] + (o - 1)
-            py = jnp.where(py < 0, py + YB, py)
-            pz = (place[2:3] + (o - 1 + nz)) % nz
-            tx = jnp.where(row_x == px, blk[3 + o:4 + o], tx)
-            ty = jnp.where(row_y == py, blk[7 + o:8 + o], ty)
-            tz = jnp.where(row_z == pz, blk[11 + o:12 + o], tz)
-        txy = jnp.concatenate([tx[i:i + 1] * ty for i in range(nx + 4)], axis=0)
-        return txy, tz
-
-    G[...] = jnp.zeros(G.shape, F32)
-    for c in range(3):
-        G[1:1 + nx, 0:ny, c * nz:(c + 1) * nz] = vel[c]
-    for d in SIDES:
-        mk[d].wait()
-
-    def dot(a, b, dims):
-        return lax.dot_general(a, b, dims, preferred_element_type=F32)
-
-    def spread(d, carry):
-        left, right = [], []
-        for k in range(2):
-            blk = mk_rx[d, k]
-            txy, tz = tables(blk)
-            left.append(txy)
-            right.append(jnp.concatenate([tz * blk[c:c + 1] for c in range(3)], axis=0))
-        left_hi, left_lo = split(jnp.concatenate(left, axis=1))
-        right_hi, right_lo = split(jnp.concatenate(right, axis=1))
-        got = dot(left_hi, right_hi, NT) + dot(left_hi, right_lo, NT) + dot(left_lo, right_hi, NT)
-        G[...] += got.reshape(G.shape)
-        return carry
-
-    lax.fori_loop(0, 9, spread, 0)
-
-    def g_row(y):
-        return y % YB
-
-    for k, (y, _) in enumerate(spread_reach(1, ny - 1)):
-        gyp_tx[k] = G[1:1 + nx, g_row(y), :]
-    for k, (y, _) in enumerate(spread_reach(-1, ny - 1)):
-        gym_tx[k] = G[1:1 + nx, g_row(y), :]
-    for i, d in enumerate(SIDES):
-        for k, (sx, sy, _, _) in enumerate(spread_corner(d, nx, ny)):
-            gc_tx[i, k] = G[sx + 1, g_row(sy):g_row(sy) + 1, :]
-    gcopies = [
-        copy(G.at[nx:nx + 3, 0:ny], gxp_rx, g_s.at[7], g_r.at[7], 7),
-        copy(G.at[0:2, 0:ny], gxm_rx, g_s.at[1], g_r.at[1], 1),
-        copy(gyp_tx, gyp_rx, g_s.at[5], g_r.at[5], 5),
-        copy(gym_tx, gym_rx, g_s.at[3], g_r.at[3], 3),
-    ]
-    for i, d in enumerate(SIDES):
-        n = len(spread_corner(d, nx, ny))
-        gcopies.append(copy(gc_tx.at[i, 0:n], gc_rx.at[i, 0:n], g_s.at[9 + i], g_r.at[9 + i], d))
-    for c in gcopies:
-        c.start()
     src[...] = jnp.zeros(src.shape, F32)
     for c in range(3):
         z = slice(c * nz, (c + 1) * nz)
@@ -331,7 +348,7 @@
                 src[c, 1 + x, 1 + y:2 + y, :] += gc_rx[i, k, :, z]
         src[c] = src[c] * inv[...]
 
-    def update(first, last, low, high, colour):
+    def update(planes, low, high, colour):
         rows = high - low
         parity = (
             lax.broadcasted_iota(jnp.int32, (rows, nz), 0)
@@ -340,7 +357,7 @@
         ) % 2
         a, b = R0 + low, R0 + high
         p, q = 1 + low, 1 + high
-        for x in range(first, last):
+        for x in planes:
             chosen = parity == (colour + x) % 2
             coef = [C[k, x + 1, p:q, :] for k in range(6)]
             for c in range(3):
@@ -357,13 +374,23 @@
                 S[c, x + 2, a:b, :] = jnp.where(chosen, new, mid)
 
     def sweep(r, carry):
-        take_state(lax.rem(r, 2))
-        update(-1, nx + 1, -1, 23, 0)
-        update(0, nx, 0, ny, 1)
+        now, later = lax.rem(r, 2), lax.rem(r + 1, 2)
+        edge = [0, 1, nx - 2, nx - 1]
+        take_y(now)
+        update(range(1, nx - 1), -1, 23, 0)
+        take_x(now)
+        update([-1, 0, nx - 1, nx], -1, 23, 0)
+        update(edge, 0, ny, 1)
 
         @pl.when(r < SWEEPS - 1)
         def _():
-            send_state(lax.rem(r + 1, 2))
+            send_x(later)
+
+        update(range(2, nx - 2), 0, ny, 1)
+
+        @pl.when(r < SWEEPS - 1)
+        def _():
+            send_y(later)
 
         return carry
 
@@ -422,13 +449,21 @@
         return carry
 
     ret_tx[...] = jnp.zeros(ret_tx.shape, F32)
-    lax.fori_loop(0, 9, sample, 0)
-    back = [copy(ret_tx.at[d], ret_rx.at[d], ret_s.at[d], ret_r.at[d], d, -1) for d in SIDES]
-    for c in back:
-        c.start()
+
+    def give_back(d):
+        return copy(ret_tx.at[d], ret_rx.at[d], ret_s.at[d], ret_r.at[d], d, -1)
+
+    def sample_side(d, carry):
+        sample(d, carry)
+        give_back(d).start()
+        return carry
+
+    lax.fori_loop(0, 4, sample_side, 0)
+    lax.fori_loop(5, 9, sample_side, 0)
+    lax.fori_loop(4, 5, sample, 0)
     ret_rx[4] = ret_tx[4]
-    for c in back:
-        c.wait()
+    for d in SIDES:
+        give_back(d).wait()
     for b in range(blocks):
         mvel[b] = ret_rx[jnp.clip(going[b], 0, 8), jnp.clip(rank[b], 0, 1)][0:3]
 

time: 78 us -> 71.5 us (0.917)
  Pallas kernels: 72.4 us -> 66 us
    pallas_call x1, Pallas kernels: 72.4 us -> 66 us  [local(): pl.pallas_call(functools.partial(kernel, size_x, size_y), out_shape=(jax....]
where the time goes in v2:
time: 71.5 us; the launch traced here: 71.2 us
  Pallas kernels  66 us (92%)
  local copies, waits for them, and re-layouts  4.51 us (6%)
    pallas_call x1, Pallas kernels, local(): pl.pallas_call(functools.partial(kernel, size_x, size_y), out_shape=(jax....  66 us
    unnamed x13, local copies, waits for them, and re-layouts  3.91 us

profile of v2, /device:TPU:1, one launch (start us, length us, event | category | flops | bytes accessed | tf_op | source)
XLA Modules:
  0.0 71.2 jit_solution(9488003676266459700)
XLA Ops:
  0.6 0.0 copy-start.2
  0.6 0.7 %copy.9.force = f32[8,3,128]{2,1,0:T(4,128)S(1)} copy(f32[8,3,128]{2,0,1:T(8,128)} %param.9) | data formatting | bytes 24576 | tf_op args[2]
  1.4 0.0 copy-start.3
  1.4 0.0 copy-start.4
  1.4 0.7 %copy.10.cells = s32[8,3,128]{2,1,0:T(4,128)S(1)} copy(s32[8,3,128]{2,0,1:T(8,128)} %param.11) | data formatting | bytes 24576 | tf_op args[4]
  2.1 0.0 copy-done.2
  2.1 0.0 copy-done.3
  2.1 0.0 copy-done.4
  2.1 0.0 copy-start
  2.1 0.9 %copy-done = f32[3,8,16,128]{3,2,1,0:T(8,128)S(1)} copy-done((f32[3,8,16,128]{3,2,1,0:T(8,128)S(1)}, f32[3,8,16,128]{3,2,1,0:T(8,128)}, u32[]{:S(2)}) %copy-start) | copy-done | bytes 196632
  3.1 0.0 copy-start.1
  3.1 0.8 %copy-done.1 = f32[8,16,128]{2,1,0:T(8,128)S(1)} copy-done((f32[8,16,128]{2,1,0:T(8,128)S(1)}, f32[8,16,128]{2,1,0:T(8,128)}, u32[]{:S(2)}) %copy-start.1) | copy-done | bytes 65560
  3.9 66.0 %shard_map.86 = (f32[3,8,16,128]{3,2,1,0:T(8,128)S(1)}, f32[8,3,128]{2,1,0:T(4,128)S(1)}) custom-call(f32[3,8,16,128]{3,2,1,0:T(8,128)S(1)} %copy-done, f32[8,16,128]{2,1,0:T(8,128)S(1)} %copy-done.1, f32[8,3,128]{2,1,0:T(4,128)S(1)} %copy.9.force, f32[8,3,4,128]{3,2,1,0:T(4,128)S(1)} %copy-done.2, s32[8,3,128]{2,1,0:T(4,128)S(1)} %copy.10.cells, ...), custom_call_target="tpu_custom_call" | custom-call | tf_op jit(solution)/shard_map/pallas_call | solution.py:508
  69.9 0.6 copy.11
  70.5 0.7 copy.13
Async XLA Ops:
  0.6 1.5 %copy-start.2 = (f32[8,3,4,128]{3,2,1,0:T(4,128)S(1)}, f32[8,3,4,128]{3,2,1,0:T(4,128)}, u32[]{:S(2)}) copy-start(f32[8,3,4,128]{3,2,1,0:T(4,128)} %weights.1) | copy-start | bytes 147460
  1.4 0.7 %copy-start.3 = (s32[8]{0:T(128)S(1)}, s32[8]{0:T(128)}, u32[]{:S(2)}) copy-start(s32[8]{0:T(128)} %count.1) | copy-start | bytes 100
  1.4 0.8 %copy-start.4 = (s32[8]{0:T(128)S(1)}, s32[8]{0:T(128)}, u32[]{:S(2)}) copy-start(s32[8]{0:T(128)} %dest.1) | copy-start | bytes 100
  2.1 0.9 %copy-start = (f32[3,8,16,128]{3,2,1,0:T(8,128)S(1)}, f32[3,8,16,128]{3,2,1,0:T(8,128)}, u32[]{:S(2)}) copy-start(f32[3,8,16,128]{3,2,1,0:T(8,128)} %vel.1) | copy-start | bytes 589828
  3.1 0.8 %copy-start.1 = (f32[8,16,128]{2,1,0:T(8,128)S(1)}, f32[8,16,128]{2,1,0:T(8,128)}, u32[]{:S(2)}) copy-start(f32[8,16,128]{2,1,0:T(8,128)} %visc.1) | copy-start | bytes 196612

commit v3 on v2

--- a/solution.py
+++ b/solution.py
@@ -273,6 +273,12 @@
     def g_row(y):
         return y % YB
 
+    gcopies = [
+        copy(G.at[nx:nx + 3, 0:ny], gxp_rx, g_s.at[7], g_r.at[7], 7),
+        copy(G.at[0:2, 0:ny], gxm_rx, g_s.at[1], g_r.at[1], 1),
+    ]
+    for c in gcopies:
+        c.start()
     for k, (y, _) in enumerate(spread_reach(1, ny - 1)):
         gyp_tx[k] = G[1:1 + nx, g_row(y), :]
     for k, (y, _) in enumerate(spread_reach(-1, ny - 1)):
@@ -280,16 +286,14 @@
     for i, d in enumerate(SIDES):
         for k, (sx, sy, _, _) in enumerate(spread_corner(d, nx, ny)):
             gc_tx[i, k] = G[sx + 1, g_row(sy):g_row(sy) + 1, :]
-    gcopies = [
-        copy(G.at[nx:nx + 3, 0:ny], gxp_rx, g_s.at[7], g_r.at[7], 7),
-        copy(G.at[0:2, 0:ny], gxm_rx, g_s.at[1], g_r.at[1], 1),
+    gcopies += [
         copy(gyp_tx, gyp_rx, g_s.at[5], g_r.at[5], 5),
         copy(gym_tx, gym_rx, g_s.at[3], g_r.at[3], 3),
     ]
     for i, d in enumerate(SIDES):
         n = len(spread_corner(d, nx, ny))
         gcopies.append(copy(gc_tx.at[i, 0:n], gc_rx.at[i, 0:n], g_s.at[9 + i], g_r.at[9 + i], d))
-    for c in gcopies:
+    for c in gcopies[2:]:
         c.start()
     V[...] = jnp.zeros(V.shape, F32)
     V[2:2 + nx, R0:R0 + ny, :] = visc[...]
@@ -398,6 +402,13 @@
 
     for c in range(3):
         flow[c] = S[c, 2:2 + nx, R0:R0 + ny, :]
+    fcopies = [
+        copy(flow.at[:, nx - 1:nx], fxp_rx, f_s.at[7], f_r.at[7], 7),
+        copy(flow.at[:, 0:2], fxm_rx, f_s.at[1], f_r.at[1], 1),
+    ]
+    for c in fcopies:
+        c.start()
+    for c in range(3):
         for k, (y, _) in enumerate(flow_reach(1, ny - 1)):
             fyp_tx[k, c] = S[c, 2:2 + nx, R0 + y, :]
         for k, (y, _) in enumerate(flow_reach(-1, ny - 1)):
@@ -405,16 +416,14 @@
         for i, d in enumerate(CORNERS):
             for k, (sx, sy, _, _) in enumerate(flow_corner(d, nx, ny)):
                 fc_tx[i, 3 * k + c] = S[c, 2 + sx, R0 + sy:R0 + sy + 1, :]
-    fcopies = [
-        copy(flow.at[:, nx - 1:nx], fxp_rx, f_s.at[7], f_r.at[7], 7),
-        copy(flow.at[:, 0:2], fxm_rx, f_s.at[1], f_r.at[1], 1),
+    fcopies += [
         copy(fyp_tx, fyp_rx, f_s.at[5], f_r.at[5], 5),
         copy(fym_tx, fym_rx, f_s.at[3], f_r.at[3], 3),
     ]
     for i, d in enumerate(CORNERS):
         n = 3 * len(flow_corner(d, nx, ny))
         fcopies.append(copy(fc_tx.at[i, 0:n], fc_rx.at[i, 0:n], f_s.at[d], f_r.at[d], d))
-    for c in fcopies:
+    for c in fcopies[2:]:
         c.start()
     fld[...] = jnp.zeros(fld.shape, F32)
     for c in range(3):

time: 71.5 us -> 71.5 us (level)
  no operation moved by 1% of the time
where the time goes in v3:
time: 71.5 us; the launch traced here: 71.2 us
  Pallas kernels  66 us (92%)
  local copies, waits for them, and re-layouts  4.51 us (6%)
    pallas_call x1, Pallas kernels, local(): pl.pallas_call(functools.partial(kernel, size_x, size_y), out_shape=(jax....  66 us
    unnamed x13, local copies, waits for them, and re-layouts  3.91 us

profile of v3, /device:TPU:1, one launch (start us, length us, event | category | flops | bytes accessed | tf_op | source)
XLA Modules:
  0.0 71.2 jit_solution(12098713364661039415)
XLA Ops:
  0.6 0.0 copy-start.2
  0.6 0.7 %copy.9.force = f32[8,3,128]{2,1,0:T(4,128)S(1)} copy(f32[8,3,128]{2,0,1:T(8,128)} %param.9) | data formatting | bytes 24576 | tf_op args[2]
  1.4 0.0 copy-start.3
  1.4 0.0 copy-start.4
  1.4 0.7 %copy.10.cells = s32[8,3,128]{2,1,0:T(4,128)S(1)} copy(s32[8,3,128]{2,0,1:T(8,128)} %param.11) | data formatting | bytes 24576 | tf_op args[4]
  2.1 0.0 copy-done.2
  2.1 0.0 copy-done.3
  2.1 0.0 copy-done.4
  2.1 0.0 copy-start
  2.1 0.9 %copy-done = f32[3,8,16,128]{3,2,1,0:T(8,128)S(1)} copy-done((f32[3,8,16,128]{3,2,1,0:T(8,128)S(1)}, f32[3,8,16,128]{3,2,1,0:T(8,128)}, u32[]{:S(2)}) %copy-start) | copy-done | bytes 196632
  3.1 0.0 copy-start.1
  3.1 0.8 %copy-done.1 = f32[8,16,128]{2,1,0:T(8,128)S(1)} copy-done((f32[8,16,128]{2,1,0:T(8,128)S(1)}, f32[8,16,128]{2,1,0:T(8,128)}, u32[]{:S(2)}) %copy-start.1) | copy-done | bytes 65560
  3.9 66.0 %shard_map.86 = (f32[3,8,16,128]{3,2,1,0:T(8,128)S(1)}, f32[8,3,128]{2,1,0:T(4,128)S(1)}) custom-call(f32[3,8,16,128]{3,2,1,0:T(8,128)S(1)} %copy-done, f32[8,16,128]{2,1,0:T(8,128)S(1)} %copy-done.1, f32[8,3,128]{2,1,0:T(4,128)S(1)} %copy.9.force, f32[8,3,4,128]{3,2,1,0:T(4,128)S(1)} %copy-done.2, s32[8,3,128]{2,1,0:T(4,128)S(1)} %copy.10.cells, ...), custom_call_target="tpu_custom_call" | custom-call | tf_op jit(solution)/shard_map/pallas_call | solution.py:517
  69.9 0.6 copy.11
  70.5 0.7 copy.13
Async XLA Ops:
  0.6 1.5 %copy-start.2 = (f32[8,3,4,128]{3,2,1,0:T(4,128)S(1)}, f32[8,3,4,128]{3,2,1,0:T(4,128)}, u32[]{:S(2)}) copy-start(f32[8,3,4,128]{3,2,1,0:T(4,128)} %weights.1) | copy-start | bytes 147460
  1.4 0.7 %copy-start.3 = (s32[8]{0:T(128)S(1)}, s32[8]{0:T(128)}, u32[]{:S(2)}) copy-start(s32[8]{0:T(128)} %count.1) | copy-start | bytes 100
  1.4 0.8 %copy-start.4 = (s32[8]{0:T(128)S(1)}, s32[8]{0:T(128)}, u32[]{:S(2)}) copy-start(s32[8]{0:T(128)} %dest.1) | copy-start | bytes 100
  2.1 0.9 %copy-start = (f32[3,8,16,128]{3,2,1,0:T(8,128)S(1)}, f32[3,8,16,128]{3,2,1,0:T(8,128)}, u32[]{:S(2)}) copy-start(f32[3,8,16,128]{3,2,1,0:T(8,128)} %vel.1) | copy-start | bytes 589828
  3.1 0.8 %copy-start.1 = (f32[8,16,128]{2,1,0:T(8,128)S(1)}, f32[8,16,128]{2,1,0:T(8,128)}, u32[]{:S(2)}) copy-start(f32[8,16,128]{2,1,0:T(8,128)} %visc.1) | copy-start | bytes 196612
